TPU v7x, 256 devices: a whole 4x4x8 slice. The times are simulated.
256 devices in a mesh: row: 8 (over z), col: 16 (over x_hi, y, core), depth: 2 (over x_lo).
Axes of the slice: x: 4 (x_hi: 2, x_lo: 2; x = x_hi * 2 + x_lo), y: 4, z: 8, core: 2. Of those that a mesh axis runs over, the one named last changes fastest.
Arguments:
- a_matrix: bfloat16 [8192, 8192], P('col', 'row'), may hold values from -6 to 6
- b_matrix: bfloat16 [8192, 14336], P('col', 'row'), may hold values from -0.0625 to 0.0625
Outputs:
- product: bfloat16 [8192, 14336], P('col', ('row', 'depth'))
All inputs are finite; a program needn't handle non-finite values.
Results may differ from a plain program's by a relative error of at most 0.0052.
Values may be sent and summed in bfloat16 or wider, within the bound.
No kernel may reach another device: no remote copies, remote signals or barrier semaphores. Data moves between devices by JAX's collectives and lax.ppermute only.
A program may use at most 64 MiB of HBM per device.

v0:
```python
import jax
import jax.numpy as jnp
from jax import lax
from jax.sharding import PartitionSpec as P


def shifted_2(value, axis, steps):
    count = lax.axis_size(axis)
    pairs = [(source, (source + steps) % count) for source in range(count)]
    return lax.ppermute(value, axis, pairs)


def body(a_matrix, b_matrix):
    row_count = lax.axis_size("row")
    col_count = lax.axis_size("col")
    depth_count = lax.axis_size("depth")
    stride = col_count // row_count
    per_device = depth_count // stride
    block_width = a_matrix.shape[1] // depth_count
    depth_index = lax.axis_index("depth")
    row_index = lax.axis_index("row")
    col_index = lax.axis_index("col")
    a_layer = lax.dynamic_slice_in_dim(a_matrix, depth_index * block_width, block_width, 1)
    b_layer = b_matrix
    running = jnp.zeros((a_matrix.shape[0], b_matrix.shape[1]), jnp.float32)
    a_offset = col_index // stride
    for bit_index in range((row_count - 1).bit_length()):
        shifted = shifted_2(a_layer, "row", -(1 << bit_index))
        a_layer = jnp.where(a_offset // (1 << bit_index) % 2 == 1, shifted, a_layer)
    b_offset = (stride * row_index + depth_index // per_device - col_index % stride) % col_count
    for bit_index in range((col_count - 1).bit_length()):
        shifted = shifted_2(b_layer, "col", -(1 << bit_index))
        b_layer = jnp.where(b_offset // (1 << bit_index) % 2 == 1, shifted, b_layer)

    def advance(step_index, state_tuple):
        left_block, right_block, summed = state_tuple
        summed = summed + jnp.dot(left_block, right_block, preferred_element_type=jnp.float32)
        left_block = shifted_2(left_block, "row", -1)
        right_block = shifted_2(right_block, "col", -stride)
        return (left_block, right_block, summed)

    a_layer, b_layer, running = lax.fori_loop(
        0, row_count - 1, advance, (a_layer, b_layer, running)
    )
    running = running + jnp.dot(a_layer, b_layer, preferred_element_type=jnp.float32)
    reduced = lax.psum_scatter(
        running.astype(jnp.bfloat16), "depth", scatter_dimension=1, tiled=True
    )
    return reduced


def solution(mesh):
    in_specs = (P("col", "row"), P("col", "row"))
    out_specs = P("col", ("row", "depth"))
    return jax.shard_map(body, mesh=mesh, in_specs=in_specs, out_specs=out_specs, check_vma=False)
```

profile of v0, /device:TPU:1, one launch (start us, length us, event | category | flops | bytes accessed | tf_op | source)
XLA Modules:
  0.0 553.4 jit_solution(14513592698762674269)
XLA Ops:
  6.5 3.2 collective-permute-start.5
  9.8 20.7 %collective-permute-done.5 = bf16[512,1792]{1,0:T(8,128)(2,1)} collective-permute-done((bf16[512,1792]{1,0:T(8,128)(2,1)}, bf16[512,1792]{1,0:T(8,128)(2,1)}, u32[]{:S(2)}, u32[]{:S(2)}) %collective-permute-start.5) | collective-permute-done | bytes 1835040 | tf_op jit(solution)/shard_map/ppermute | solution.py:10
  32.2 8.8 %collective-permute-start.6 = (bf16[512,1792]{1,0:T(8,128)(2,1)S(1)}, bf16[512,1792]{1,0:T(8,128)(2,1)}, u32[]{:S(2)}, u32[]{:S(2)}) collective-permute-start(bf16[512,1792]{1,0:T(8,128)(2,1)S(1)} %broadcast_select_fusion), channel_id=1, source_target_pairs={{0,28},{2,30},{4,0},{6,2},{8,4},{10,6},{12,8},{14,10},{16,12},{18,... | collective-permute-start | bytes 5505032 | tf_op jit(solution)/shard_map/ppermute | solution.py:10
  40.9 35.6 %collective-permute-done.6 = bf16[512,1792]{1,0:T(8,128)(2,1)} collective-permute-done((bf16[512,1792]{1,0:T(8,128)(2,1)S(1)}, bf16[512,1792]{1,0:T(8,128)(2,1)}, u32[]{:S(2)}, u32[]{:S(2)}) %collective-permute-start.6) | collective-permute-done | bytes 1835040 | tf_op jit(solution)/shard_map/ppermute | solution.py:10
  80.4 5.7 %collective-permute-start.2 = (bf16[512,512]{1,0:T(8,128)(2,1)S(1)}, bf16[512,512]{1,0:T(8,128)(2,1)S(1)}, u32[]{:S(2)}, u32[]{:S(2)}) collective-permute-start(bf16[512,512]{1,0:T(8,128)(2,1)S(1)} %constant_dynamic-slice_fusion), channel_id=1, source_target_pairs={{0,224},{32,0},{64,32},{96,64},{128,96},{160,128},{192,160},{224,1... | collective-permute-start | bytes 1572872 | tf_op jit(solution)/shard_map/ppermute | solution.py:10
  86.0 34.3 %collective-permute-done.7 = bf16[512,1792]{1,0:T(8,128)(2,1)} collective-permute-done((bf16[512,1792]{1,0:T(8,128)(2,1)S(1)}, bf16[512,1792]{1,0:T(8,128)(2,1)}, u32[]{:S(2)}, u32[]{:S(2)}) %collective-permute-start.7) | collective-permute-done | bytes 1835040 | tf_op jit(solution)/shard_map/ppermute | solution.py:10
  124.0 6.1 %collective-permute-start.3 = (bf16[512,512]{1,0:T(8,128)(2,1)S(1)}, bf16[512,512]{1,0:T(8,128)(2,1)S(1)}, u32[]{:S(2)}, u32[]{:S(2)}) collective-permute-start(bf16[512,512]{1,0:T(8,128)(2,1)S(1)} %broadcast_select_fusion.4), channel_id=1, source_target_pairs={{0,192},{32,224},{64,0},{96,32},{128,64},{160,96},{192,128},{224,1... | collective-permute-start | bytes 1572872 | tf_op jit(solution)/shard_map/ppermute | solution.py:10
  130.1 19.4 %collective-permute-done.3 = bf16[512,512]{1,0:T(8,128)(2,1)S(1)} collective-permute-done((bf16[512,512]{1,0:T(8,128)(2,1)S(1)}, bf16[512,512]{1,0:T(8,128)(2,1)S(1)}, u32[]{:S(2)}, u32[]{:S(2)}) %collective-permute-start.3) | collective-permute-done | bytes 524320 | tf_op jit(solution)/shard_map/ppermute | solution.py:10
  149.5 6.4 %collective-permute-start.4 = (bf16[512,512]{1,0:T(8,128)(2,1)S(1)}, bf16[512,512]{1,0:T(8,128)(2,1)S(1)}, u32[]{:S(2)}, u32[]{:S(2)}) collective-permute-start(bf16[512,512]{1,0:T(8,128)(2,1)S(1)} %broadcast_select_fusion.5), channel_id=1, source_target_pairs={{0,128},{32,160},{64,192},{96,224},{128,0},{160,32},{192,64},{224,... | collective-permute-start | bytes 1572872 | tf_op jit(solution)/shard_map/ppermute | solution.py:10
  156.0 8.7 %collective-permute-done.4 = bf16[512,512]{1,0:T(8,128)(2,1)S(1)} collective-permute-done((bf16[512,512]{1,0:T(8,128)(2,1)S(1)}, bf16[512,512]{1,0:T(8,128)(2,1)S(1)}, u32[]{:S(2)}, u32[]{:S(2)}) %collective-permute-start.4) | collective-permute-done | bytes 524320 | tf_op jit(solution)/shard_map/ppermute | solution.py:10
  165.3 2.9 broadcast_select_fusion.3
  168.3 328.3 %while.15 = (s32[]{:T(128)}, bf16[512,512]{1,0:T(8,128)(2,1)S(1)}, bf16[512,1792]{1,0:T(8,128)(2,1)}, f32[512,1792]{1,0:T(8,128)}, s32[]{:T(128)}, /*index=5*/s32[]{:T(128)}) while((s32[]{:T(128)}, bf16[512,512]{1,0:T(8,128)(2,1)S(1)}, bf16[512,1792]{1,0:T(8,128)(2,1)}, f32[512,1792]{1,0:T(8,128)}, s32[]{:T(128)}, ...), condition=%wide.region_1.2_spmd.clone, body=%wide.region_0.1_spmd.clone.sunk | while | flops 941359104 | bytes 23855264 | solution.py:42
  169.8 16.9 %collective-permute-start.1 = (bf16[512,1792]{1,0:T(8,128)(2,1)S(1)}, bf16[512,1792]{1,0:T(8,128)(2,1)}, u32[]{:S(2)}, u32[]{:S(2)}) collective-permute-start(bf16[512,1792]{1,0:T(8,128)(2,1)S(1)} %copy.11), channel_id=1, source_target_pairs={{0,28},{2,30},{4,0},{6,2},{8,4},{10,6},{12,8},{14,10},{16,12},{18,... | collective-permute-start | bytes 5505032 | tf_op jit(solution)/shard_map/while/body/eval_jaxpr/ppermute | solution.py:10
  186.7 5.6 %collective-permute-start = (bf16[512,512]{1,0:T(8,128)(2,1)S(1)}, bf16[512,512]{1,0:T(8,128)(2,1)S(1)}, u32[]{:S(2)}, u32[]{:S(2)}) collective-permute-start(bf16[512,512]{1,0:T(8,128)(2,1)S(1)} %copy.10), channel_id=1, source_target_pairs={{0,224},{32,0},{64,32},{96,64},{128,96},{160,128},{192,160},{224,1... | collective-permute-start | bytes 1572872 | tf_op jit(solution)/shard_map/while/body/eval_jaxpr/ppermute | solution.py:10
  192.3 2.9 select_add_fusion.2
  195.2 7.5 %collective-permute-done = bf16[512,512]{1,0:T(8,128)(2,1)S(1)} collective-permute-done((bf16[512,512]{1,0:T(8,128)(2,1)S(1)}, bf16[512,512]{1,0:T(8,128)(2,1)S(1)}, u32[]{:S(2)}, u32[]{:S(2)}) %collective-permute-start) | collective-permute-done | bytes 524320 | tf_op jit(solution)/shard_map/while/body/eval_jaxpr/ppermute | solution.py:10
  202.8 21.9 %collective-permute-done.1 = bf16[512,1792]{1,0:T(8,128)(2,1)} collective-permute-done((bf16[512,1792]{1,0:T(8,128)(2,1)S(1)}, bf16[512,1792]{1,0:T(8,128)(2,1)}, u32[]{:S(2)}, u32[]{:S(2)}) %collective-permute-start.1) | collective-permute-done | bytes 1835040 | tf_op jit(solution)/shard_map/while/body/eval_jaxpr/ppermute | solution.py:10
  226.2 4.0 collective-permute-start.1
  230.3 8.4 %collective-permute-start = (bf16[512,512]{1,0:T(8,128)(2,1)S(1)}, bf16[512,512]{1,0:T(8,128)(2,1)S(1)}, u32[]{:S(2)}, u32[]{:S(2)}) collective-permute-start(bf16[512,512]{1,0:T(8,128)(2,1)S(1)} %copy.10), channel_id=1, source_target_pairs={{0,224},{32,0},{64,32},{96,64},{128,96},{160,128},{192,160},{224,1... | collective-permute-start | bytes 1572872 | tf_op jit(solution)/shard_map/while/body/eval_jaxpr/ppermute | solution.py:10
  238.6 5.0 select_add_fusion.2
  243.6 4.6 collective-permute-done
  248.2 19.5 %collective-permute-done.1 = bf16[512,1792]{1,0:T(8,128)(2,1)} collective-permute-done((bf16[512,1792]{1,0:T(8,128)(2,1)S(1)}, bf16[512,1792]{1,0:T(8,128)(2,1)}, u32[]{:S(2)}, u32[]{:S(2)}) %collective-permute-start.1) | collective-permute-done | bytes 1835040 | tf_op jit(solution)/shard_map/while/body/eval_jaxpr/ppermute | solution.py:10
  269.2 5.6 %collective-permute-start.1 = (bf16[512,1792]{1,0:T(8,128)(2,1)S(1)}, bf16[512,1792]{1,0:T(8,128)(2,1)}, u32[]{:S(2)}, u32[]{:S(2)}) collective-permute-start(bf16[512,1792]{1,0:T(8,128)(2,1)S(1)} %copy.11), channel_id=1, source_target_pairs={{0,28},{2,30},{4,0},{6,2},{8,4},{10,6},{12,8},{14,10},{16,12},{18,... | collective-permute-start | bytes 5505032 | tf_op jit(solution)/shard_map/while/body/eval_jaxpr/ppermute | solution.py:10
  274.9 9.1 %collective-permute-start = (bf16[512,512]{1,0:T(8,128)(2,1)S(1)}, bf16[512,512]{1,0:T(8,128)(2,1)S(1)}, u32[]{:S(2)}, u32[]{:S(2)}) collective-permute-start(bf16[512,512]{1,0:T(8,128)(2,1)S(1)} %copy.10), channel_id=1, source_target_pairs={{0,224},{32,0},{64,32},{96,64},{128,96},{160,128},{192,160},{224,1... | collective-permute-start | bytes 1572872 | tf_op jit(solution)/shard_map/while/body/eval_jaxpr/ppermute | solution.py:10
  284.0 5.0 select_add_fusion.2
  289.0 3.7 collective-permute-done
  292.7 20.8 %collective-permute-done.1 = bf16[512,1792]{1,0:T(8,128)(2,1)} collective-permute-done((bf16[512,1792]{1,0:T(8,128)(2,1)S(1)}, bf16[512,1792]{1,0:T(8,128)(2,1)}, u32[]{:S(2)}, u32[]{:S(2)}) %collective-permute-start.1) | collective-permute-done | bytes 1835040 | tf_op jit(solution)/shard_map/while/body/eval_jaxpr/ppermute | solution.py:10
  314.9 5.6 %collective-permute-start.1 = (bf16[512,1792]{1,0:T(8,128)(2,1)S(1)}, bf16[512,1792]{1,0:T(8,128)(2,1)}, u32[]{:S(2)}, u32[]{:S(2)}) collective-permute-start(bf16[512,1792]{1,0:T(8,128)(2,1)S(1)} %copy.11), channel_id=1, source_target_pairs={{0,28},{2,30},{4,0},{6,2},{8,4},{10,6},{12,8},{14,10},{16,12},{18,... | collective-permute-start | bytes 5505032 | tf_op jit(solution)/shard_map/while/body/eval_jaxpr/ppermute | solution.py:10
  320.6 7.9 %collective-permute-start = (bf16[512,512]{1,0:T(8,128)(2,1)S(1)}, bf16[512,512]{1,0:T(8,128)(2,1)S(1)}, u32[]{:S(2)}, u32[]{:S(2)}) collective-permute-start(bf16[512,512]{1,0:T(8,128)(2,1)S(1)} %copy.10), channel_id=1, source_target_pairs={{0,224},{32,0},{64,32},{96,64},{128,96},{160,128},{192,160},{224,1... | collective-permute-start | bytes 1572872 | tf_op jit(solution)/shard_map/while/body/eval_jaxpr/ppermute | solution.py:10
  328.5 5.0 select_add_fusion.2
  333.4 2.8 collective-permute-done
  336.2 24.1 %collective-permute-done.1 = bf16[512,1792]{1,0:T(8,128)(2,1)} collective-permute-done((bf16[512,1792]{1,0:T(8,128)(2,1)S(1)}, bf16[512,1792]{1,0:T(8,128)(2,1)}, u32[]{:S(2)}, u32[]{:S(2)}) %collective-permute-start.1) | collective-permute-done | bytes 1835040 | tf_op jit(solution)/shard_map/while/body/eval_jaxpr/ppermute | solution.py:10
  361.8 5.7 %collective-permute-start.1 = (bf16[512,1792]{1,0:T(8,128)(2,1)S(1)}, bf16[512,1792]{1,0:T(8,128)(2,1)}, u32[]{:S(2)}, u32[]{:S(2)}) collective-permute-start(bf16[512,1792]{1,0:T(8,128)(2,1)S(1)} %copy.11), channel_id=1, source_target_pairs={{0,28},{2,30},{4,0},{6,2},{8,4},{10,6},{12,8},{14,10},{16,12},{18,... | collective-permute-start | bytes 5505032 | tf_op jit(solution)/shard_map/while/body/eval_jaxpr/ppermute | solution.py:10
  367.5 4.4 collective-permute-start
  372.0 5.0 select_add_fusion.2
  376.9 3.6 collective-permute-done
  380.5 26.0 %collective-permute-done.1 = bf16[512,1792]{1,0:T(8,128)(2,1)} collective-permute-done((bf16[512,1792]{1,0:T(8,128)(2,1)S(1)}, bf16[512,1792]{1,0:T(8,128)(2,1)}, u32[]{:S(2)}, u32[]{:S(2)}) %collective-permute-start.1) | collective-permute-done | bytes 1835040 | tf_op jit(solution)/shard_map/while/body/eval_jaxpr/ppermute | solution.py:10
  408.0 5.9 %collective-permute-start.1 = (bf16[512,1792]{1,0:T(8,128)(2,1)S(1)}, bf16[512,1792]{1,0:T(8,128)(2,1)}, u32[]{:S(2)}, u32[]{:S(2)}) collective-permute-start(bf16[512,1792]{1,0:T(8,128)(2,1)S(1)} %copy.11), channel_id=1, source_target_pairs={{0,28},{2,30},{4,0},{6,2},{8,4},{10,6},{12,8},{14,10},{16,12},{18,... | collective-permute-start | bytes 5505032 | tf_op jit(solution)/shard_map/while/body/eval_jaxpr/ppermute | solution.py:10
  414.6 5.0 select_add_fusion.2
  419.6 6.5 %collective-permute-done = bf16[512,512]{1,0:T(8,128)(2,1)S(1)} collective-permute-done((bf16[512,512]{1,0:T(8,128)(2,1)S(1)}, bf16[512,512]{1,0:T(8,128)(2,1)S(1)}, u32[]{:S(2)}, u32[]{:S(2)}) %collective-permute-start) | collective-permute-done | bytes 524320 | tf_op jit(solution)/shard_map/while/body/eval_jaxpr/ppermute | solution.py:10
  426.1 25.9 %collective-permute-done.1 = bf16[512,1792]{1,0:T(8,128)(2,1)} collective-permute-done((bf16[512,1792]{1,0:T(8,128)(2,1)S(1)}, bf16[512,1792]{1,0:T(8,128)(2,1)}, u32[]{:S(2)}, u32[]{:S(2)}) %collective-permute-start.1) | collective-permute-done | bytes 1835040 | tf_op jit(solution)/shard_map/while/body/eval_jaxpr/ppermute | solution.py:10
  453.5 5.9 %collective-permute-start.1 = (bf16[512,1792]{1,0:T(8,128)(2,1)S(1)}, bf16[512,1792]{1,0:T(8,128)(2,1)}, u32[]{:S(2)}, u32[]{:S(2)}) collective-permute-start(bf16[512,1792]{1,0:T(8,128)(2,1)S(1)} %copy.11), channel_id=1, source_target_pairs={{0,28},{2,30},{4,0},{6,2},{8,4},{10,6},{12,8},{14,10},{16,12},{18,... | collective-permute-start | bytes 5505032 | tf_op jit(solution)/shard_map/while/body/eval_jaxpr/ppermute | solution.py:10
  459.6 5.0 select_add_fusion.2
  464.5 6.1 %collective-permute-done = bf16[512,512]{1,0:T(8,128)(2,1)S(1)} collective-permute-done((bf16[512,512]{1,0:T(8,128)(2,1)S(1)}, bf16[512,512]{1,0:T(8,128)(2,1)S(1)}, u32[]{:S(2)}, u32[]{:S(2)}) %collective-permute-start) | collective-permute-done | bytes 524320 | tf_op jit(solution)/shard_map/while/body/eval_jaxpr/ppermute | solution.py:10
  470.6 25.9 %collective-permute-done.1 = bf16[512,1792]{1,0:T(8,128)(2,1)} collective-permute-done((bf16[512,1792]{1,0:T(8,128)(2,1)S(1)}, bf16[512,1792]{1,0:T(8,128)(2,1)}, u32[]{:S(2)}, u32[]{:S(2)}) %collective-permute-start.1) | collective-permute-done | bytes 1835040 | tf_op jit(solution)/shard_map/while/body/eval_jaxpr/ppermute | solution.py:10
  496.6 2.8 fusion
  499.8 2.4 copy.3
  502.2 42.1 %reduce-scatter.4.cloned.1.call-done = bf16[896,512]{1,0:T(8,128)(2,1)} async-done(((bf16[1792,512]{1,0:T(8,128)(2,1)}), bf16[896,512]{1,0:T(8,128)(2,1)}) %reduce-scatter.4.cloned.1.call-update) | async-done | bytes 917520
  (40 shorter events, 24.0 us)
Async XLA Ops:
  6.5 537.8 %reduce-scatter.4.cloned.1.call-start = ((), (), s32[]{:S(2)}) async-start(), calls=%async_computation.1 | async-start | bytes 2752512
  6.5 23.9 %collective-permute-start.5 = (bf16[512,1792]{1,0:T(8,128)(2,1)}, bf16[512,1792]{1,0:T(8,128)(2,1)}, u32[]{:S(2)}, u32[]{:S(2)}) collective-permute-start(bf16[512,1792]{1,0:T(8,128)(2,1)} %param.5), channel_id=1, source_target_pairs={{0,30},{2,0},{4,2},{6,4},{8,6},{10,8},{12,10},{14,12},{16,14},{18,... | collective-permute-start | bytes 5505032 | tf_op jit(solution)/shard_map/ppermute | solution.py:10
  32.1 8.8 %copy-start.2 = (bf16[512,1792]{1,0:T(8,128)(2,1)}, bf16[512,1792]{1,0:T(8,128)(2,1)S(1)}, u32[]{:S(2)}) copy-start(bf16[512,1792]{1,0:T(8,128)(2,1)S(1)} %broadcast_select_fusion) | copy-start | bytes 5505028
  32.2 44.4 %collective-permute-start.6 = (bf16[512,1792]{1,0:T(8,128)(2,1)S(1)}, bf16[512,1792]{1,0:T(8,128)(2,1)}, u32[]{:S(2)}, u32[]{:S(2)}) collective-permute-start(bf16[512,1792]{1,0:T(8,128)(2,1)S(1)} %broadcast_select_fusion), channel_id=1, source_target_pairs={{0,28},{2,30},{4,0},{6,2},{8,4},{10,6},{12,8},{14,10},{16,12},{18,... | collective-permute-start | bytes 5505032 | tf_op jit(solution)/shard_map/ppermute | solution.py:10
  40.9 39.4 %copy-start.3 = (bf16[512,1024]{1,0:T(8,128)(2,1)S(1)}, bf16[512,1024]{1,0:T(8,128)(2,1)}, u32[]{:S(2)}) copy-start(bf16[512,1024]{1,0:T(8,128)(2,1)} %param.4) | copy-start | bytes 3145732
  78.3 7.8 %copy-start.1 = (bf16[512,1792]{1,0:T(8,128)(2,1)}, bf16[512,1792]{1,0:T(8,128)(2,1)S(1)}, u32[]{:S(2)}) copy-start(bf16[512,1792]{1,0:T(8,128)(2,1)S(1)} %broadcast_select_fusion.1) | copy-start | bytes 5505028
  78.3 42.1 %collective-permute-start.7 = (bf16[512,1792]{1,0:T(8,128)(2,1)S(1)}, bf16[512,1792]{1,0:T(8,128)(2,1)}, u32[]{:S(2)}, u32[]{:S(2)}) collective-permute-start(bf16[512,1792]{1,0:T(8,128)(2,1)S(1)} %broadcast_select_fusion.1), channel_id=1, source_target_pairs={{0,24},{2,26},{4,28},{6,30},{8,0},{10,2},{12,4},{14,6},{16,8},{18,... | collective-permute-start | bytes 5505032 | tf_op jit(solution)/shard_map/ppermute | solution.py:10
  80.4 42.4 %collective-permute-start.2 = (bf16[512,512]{1,0:T(8,128)(2,1)S(1)}, bf16[512,512]{1,0:T(8,128)(2,1)S(1)}, u32[]{:S(2)}, u32[]{:S(2)}) collective-permute-start(bf16[512,512]{1,0:T(8,128)(2,1)S(1)} %constant_dynamic-slice_fusion), channel_id=1, source_target_pairs={{0,224},{32,0},{64,32},{96,64},{128,96},{160,128},{192,160},{224,1... | collective-permute-start | bytes 1572872 | tf_op jit(solution)/shard_map/ppermute | solution.py:10
  122.1 43.3 %collective-permute-start.8 = (bf16[512,1792]{1,0:T(8,128)(2,1)S(1)}, bf16[512,1792]{1,0:T(8,128)(2,1)}, u32[]{:S(2)}, u32[]{:S(2)}) collective-permute-start(bf16[512,1792]{1,0:T(8,128)(2,1)S(1)} %broadcast_select_fusion.2), channel_id=1, source_target_pairs={{0,16},{2,18},{4,20},{6,22},{8,24},{10,26},{12,28},{14,30},{16,0},... | collective-permute-start | bytes 5505032 | tf_op jit(solution)/shard_map/ppermute | solution.py:10
  124.0 25.5 %collective-permute-start.3 = (bf16[512,512]{1,0:T(8,128)(2,1)S(1)}, bf16[512,512]{1,0:T(8,128)(2,1)S(1)}, u32[]{:S(2)}, u32[]{:S(2)}) collective-permute-start(bf16[512,512]{1,0:T(8,128)(2,1)S(1)} %broadcast_select_fusion.4), channel_id=1, source_target_pairs={{0,192},{32,224},{64,0},{96,32},{128,64},{160,96},{192,128},{224,1... | collective-permute-start | bytes 1572872 | tf_op jit(solution)/shard_map/ppermute | solution.py:10
  149.5 15.2 %collective-permute-start.4 = (bf16[512,512]{1,0:T(8,128)(2,1)S(1)}, bf16[512,512]{1,0:T(8,128)(2,1)S(1)}, u32[]{:S(2)}, u32[]{:S(2)}) collective-permute-start(bf16[512,512]{1,0:T(8,128)(2,1)S(1)} %broadcast_select_fusion.5), channel_id=1, source_target_pairs={{0,128},{32,160},{64,192},{96,224},{128,0},{160,32},{192,64},{224,... | collective-permute-start | bytes 1572872 | tf_op jit(solution)/shard_map/ppermute | solution.py:10
  169.8 55.0 %collective-permute-start.1 = (bf16[512,1792]{1,0:T(8,128)(2,1)S(1)}, bf16[512,1792]{1,0:T(8,128)(2,1)}, u32[]{:S(2)}, u32[]{:S(2)}) collective-permute-start(bf16[512,1792]{1,0:T(8,128)(2,1)S(1)} %copy.11), channel_id=1, source_target_pairs={{0,28},{2,30},{4,0},{6,2},{8,4},{10,6},{12,8},{14,10},{16,12},{18,... | collective-permute-start | bytes 5505032 | tf_op jit(solution)/shard_map/while/body/eval_jaxpr/ppermute | solution.py:10
  186.7 16.1 %collective-permute-start = (bf16[512,512]{1,0:T(8,128)(2,1)S(1)}, bf16[512,512]{1,0:T(8,128)(2,1)S(1)}, u32[]{:S(2)}, u32[]{:S(2)}) collective-permute-start(bf16[512,512]{1,0:T(8,128)(2,1)S(1)} %copy.10), channel_id=1, source_target_pairs={{0,224},{32,0},{64,32},{96,64},{128,96},{160,128},{192,160},{224,1... | collective-permute-start | bytes 1572872 | tf_op jit(solution)/shard_map/while/body/eval_jaxpr/ppermute | solution.py:10
  226.2 41.5 %collective-permute-start.1 = (bf16[512,1792]{1,0:T(8,128)(2,1)S(1)}, bf16[512,1792]{1,0:T(8,128)(2,1)}, u32[]{:S(2)}, u32[]{:S(2)}) collective-permute-start(bf16[512,1792]{1,0:T(8,128)(2,1)S(1)} %copy.11), channel_id=1, source_target_pairs={{0,28},{2,30},{4,0},{6,2},{8,4},{10,6},{12,8},{14,10},{16,12},{18,... | collective-permute-start | bytes 5505032 | tf_op jit(solution)/shard_map/while/body/eval_jaxpr/ppermute | solution.py:10
  230.3 17.9 %collective-permute-start = (bf16[512,512]{1,0:T(8,128)(2,1)S(1)}, bf16[512,512]{1,0:T(8,128)(2,1)S(1)}, u32[]{:S(2)}, u32[]{:S(2)}) collective-permute-start(bf16[512,512]{1,0:T(8,128)(2,1)S(1)} %copy.10), channel_id=1, source_target_pairs={{0,224},{32,0},{64,32},{96,64},{128,96},{160,128},{192,160},{224,1... | collective-permute-start | bytes 1572872 | tf_op jit(solution)/shard_map/while/body/eval_jaxpr/ppermute | solution.py:10
  269.2 44.2 %collective-permute-start.1 = (bf16[512,1792]{1,0:T(8,128)(2,1)S(1)}, bf16[512,1792]{1,0:T(8,128)(2,1)}, u32[]{:S(2)}, u32[]{:S(2)}) collective-permute-start(bf16[512,1792]{1,0:T(8,128)(2,1)S(1)} %copy.11), channel_id=1, source_target_pairs={{0,28},{2,30},{4,0},{6,2},{8,4},{10,6},{12,8},{14,10},{16,12},{18,... | collective-permute-start | bytes 5505032 | tf_op jit(solution)/shard_map/while/body/eval_jaxpr/ppermute | solution.py:10
  274.9 17.8 %collective-permute-start = (bf16[512,512]{1,0:T(8,128)(2,1)S(1)}, bf16[512,512]{1,0:T(8,128)(2,1)S(1)}, u32[]{:S(2)}, u32[]{:S(2)}) collective-permute-start(bf16[512,512]{1,0:T(8,128)(2,1)S(1)} %copy.10), channel_id=1, source_target_pairs={{0,224},{32,0},{64,32},{96,64},{128,96},{160,128},{192,160},{224,1... | collective-permute-start | bytes 1572872 | tf_op jit(solution)/shard_map/while/body/eval_jaxpr/ppermute | solution.py:10
  314.9 45.4 %collective-permute-start.1 = (bf16[512,1792]{1,0:T(8,128)(2,1)S(1)}, bf16[512,1792]{1,0:T(8,128)(2,1)}, u32[]{:S(2)}, u32[]{:S(2)}) collective-permute-start(bf16[512,1792]{1,0:T(8,128)(2,1)S(1)} %copy.11), channel_id=1, source_target_pairs={{0,28},{2,30},{4,0},{6,2},{8,4},{10,6},{12,8},{14,10},{16,12},{18,... | collective-permute-start | bytes 5505032 | tf_op jit(solution)/shard_map/while/body/eval_jaxpr/ppermute | solution.py:10
  320.6 15.6 %collective-permute-start = (bf16[512,512]{1,0:T(8,128)(2,1)S(1)}, bf16[512,512]{1,0:T(8,128)(2,1)S(1)}, u32[]{:S(2)}, u32[]{:S(2)}) collective-permute-start(bf16[512,512]{1,0:T(8,128)(2,1)S(1)} %copy.10), channel_id=1, source_target_pairs={{0,224},{32,0},{64,32},{96,64},{128,96},{160,128},{192,160},{224,1... | collective-permute-start | bytes 1572872 | tf_op jit(solution)/shard_map/while/body/eval_jaxpr/ppermute | solution.py:10
  361.8 44.7 %collective-permute-start.1 = (bf16[512,1792]{1,0:T(8,128)(2,1)S(1)}, bf16[512,1792]{1,0:T(8,128)(2,1)}, u32[]{:S(2)}, u32[]{:S(2)}) collective-permute-start(bf16[512,1792]{1,0:T(8,128)(2,1)S(1)} %copy.11), channel_id=1, source_target_pairs={{0,28},{2,30},{4,0},{6,2},{8,4},{10,6},{12,8},{14,10},{16,12},{18,... | collective-permute-start | bytes 5505032 | tf_op jit(solution)/shard_map/while/body/eval_jaxpr/ppermute | solution.py:10
  367.5 13.0 %collective-permute-start = (bf16[512,512]{1,0:T(8,128)(2,1)S(1)}, bf16[512,512]{1,0:T(8,128)(2,1)S(1)}, u32[]{:S(2)}, u32[]{:S(2)}) collective-permute-start(bf16[512,512]{1,0:T(8,128)(2,1)S(1)} %copy.10), channel_id=1, source_target_pairs={{0,224},{32,0},{64,32},{96,64},{128,96},{160,128},{192,160},{224,1... | collective-permute-start | bytes 1572872 | tf_op jit(solution)/shard_map/while/body/eval_jaxpr/ppermute | solution.py:10
  408.0 44.0 %collective-permute-start.1 = (bf16[512,1792]{1,0:T(8,128)(2,1)S(1)}, bf16[512,1792]{1,0:T(8,128)(2,1)}, u32[]{:S(2)}, u32[]{:S(2)}) collective-permute-start(bf16[512,1792]{1,0:T(8,128)(2,1)S(1)} %copy.11), channel_id=1, source_target_pairs={{0,28},{2,30},{4,0},{6,2},{8,4},{10,6},{12,8},{14,10},{16,12},{18,... | collective-permute-start | bytes 5505032 | tf_op jit(solution)/shard_map/while/body/eval_jaxpr/ppermute | solution.py:10
  414.0 12.1 %collective-permute-start = (bf16[512,512]{1,0:T(8,128)(2,1)S(1)}, bf16[512,512]{1,0:T(8,128)(2,1)S(1)}, u32[]{:S(2)}, u32[]{:S(2)}) collective-permute-start(bf16[512,512]{1,0:T(8,128)(2,1)S(1)} %copy.10), channel_id=1, source_target_pairs={{0,224},{32,0},{64,32},{96,64},{128,96},{160,128},{192,160},{224,1... | collective-permute-start | bytes 1572872 | tf_op jit(solution)/shard_map/while/body/eval_jaxpr/ppermute | solution.py:10
  453.5 43.1 %collective-permute-start.1 = (bf16[512,1792]{1,0:T(8,128)(2,1)S(1)}, bf16[512,1792]{1,0:T(8,128)(2,1)}, u32[]{:S(2)}, u32[]{:S(2)}) collective-permute-start(bf16[512,1792]{1,0:T(8,128)(2,1)S(1)} %copy.11), channel_id=1, source_target_pairs={{0,28},{2,30},{4,0},{6,2},{8,4},{10,6},{12,8},{14,10},{16,12},{18,... | collective-permute-start | bytes 5505032 | tf_op jit(solution)/shard_map/while/body/eval_jaxpr/ppermute | solution.py:10
  459.5 11.2 %collective-permute-start = (bf16[512,512]{1,0:T(8,128)(2,1)S(1)}, bf16[512,512]{1,0:T(8,128)(2,1)S(1)}, u32[]{:S(2)}, u32[]{:S(2)}) collective-permute-start(bf16[512,512]{1,0:T(8,128)(2,1)S(1)} %copy.10), channel_id=1, source_target_pairs={{0,224},{32,0},{64,32},{96,64},{128,96},{160,128},{192,160},{224,1... | collective-permute-start | bytes 1572872 | tf_op jit(solution)/shard_map/while/body/eval_jaxpr/ppermute | solution.py:10
  496.6 2.8 copy-start
Sparse Core Ops, SparseCore 0:
  502.3 41.9 reduce-scatter.3
where the time goes:
time: 554 us; the launch traced here: 553 us
  waiting for transfers between devices  360 us (65%)
  starting transfers between devices  119 us (21%)
  matrix products  35.5 us (6%)
  local copies, waits for them, and re-layouts  15.4 us (3%)
  between operations  13.5 us (2%)
  other arithmetic  9.79 us (2%)
    ppermute x21, waiting for transfers between devices, shifted_2(): return lax.ppermute(value, axis, pairs)  318 us
    ppermute x21, starting transfers between devices, shifted_2(): return lax.ppermute(value, axis, pairs)  119 us
    unnamed x2, waiting for transfers between devices  42.1 us
    dot_general x7, matrix products, advance(): jnp.dot(left_block, right_block, preferred_element_type=jnp.float32)  32.7 us
  transfers between devices with their start and end apart: 22, of which 21 were waited for; matrix products, arithmetic and copies ran while one was open for 6% of the time, Pallas kernels for 0%

commit v1 on v0

v1 whole, which is shorter than its diff:
```python
import jax
import jax.numpy as jnp
from jax import lax
from jax.sharding import PartitionSpec as P

AXES = ("row", "col", "depth")
Z, X, Y = 8, 2, 4


def moved(value, target):
    def number(z, x_hi, y, core, x_lo):
        return (((z * X + x_hi) * Y + y) * 2 + core) * 2 + x_lo

    pairs = [
        (number(z, x_hi, y, core, x_lo), number(*target(z, x_hi, y, core, x_lo)))
        for z in range(Z) for x_hi in range(X) for y in range(Y) for core in range(2) for x_lo in range(2)
    ]
    return lax.ppermute(value, AXES, pairs)


def z_up(z, x_hi, y, core, x_lo):
    return (z + 1) % Z, x_hi, y, core, x_lo


def z_down(z, x_hi, y, core, x_lo):
    return (z - 1) % Z, x_hi, y, core, x_lo


def y_up(z, x_hi, y, core, x_lo):
    return z, x_hi, (y + 1) % Y, core, x_lo


def y_down(z, x_hi, y, core, x_lo):
    return z, x_hi, (y - 1) % Y, core, x_lo


def x_side(z, x_hi, y, core, x_lo):
    return z, 1 - x_hi, y, core, 1 - x_lo


def x_pair(z, x_hi, y, core, x_lo):
    return z, x_hi, y, core, 1 - x_lo


def sibling(z, x_hi, y, core, x_lo):
    return z, x_hi, y, 1 - core, x_lo


def body(a_matrix, b_matrix):
    rows, width = a_matrix.shape
    depth, columns = b_matrix.shape
    half = depth // 2
    z = lax.axis_index("row")
    col = lax.axis_index("col")
    x_lo = lax.axis_index("depth")
    x_hi, y, core = col // (2 * Y), col // 2 % Y, col % 2
    part = x_hi ^ x_lo

    a_view = a_matrix.reshape(rows, 2, 2, half)
    a_mine = lax.dynamic_slice(a_view, (0, core, part, 0), (rows, 1, 1, half)).reshape(rows, half)
    a_other = lax.dynamic_slice(a_view, (0, 1 - core, part, 0), (rows, 1, 1, half)).reshape(rows, half)
    piece = jnp.concatenate([a_mine, a_other], 1)
    a_pieces = [(piece, 0)]
    up = down = piece
    for step in range(1, Z // 2 + 1):
        up = moved(up, z_up)
        a_pieces.append((up, -step))
        if step < Z // 2:
            down = moved(down, z_down)
            a_pieces.append((down, step))
    left = [jnp.zeros((rows, Z * half), a_matrix.dtype) for _ in range(2)]
    for value, offset in a_pieces:
        place = (z + offset) % Z
        for k in range(2):
            left[k] = lax.dynamic_update_slice(left[k], value[:, k * half:(k + 1) * half], (0, place * half))

    own = lax.dynamic_slice(b_matrix, (part * half, 0), (half, columns))
    nb = moved(own, x_side)
    own_up = moved(own, y_up)
    own_down = moved(own, y_down)
    far_a = moved(own_up[: half // 2], y_up)
    far_b = moved(own_down[half // 2:], y_down)
    nb_up = moved(nb, y_up)
    nb_down = moved(nb, y_down)
    nb_far_a = moved(far_a, x_side)
    nb_far_b = moved(far_b, x_side)
    b_pieces = [(own, 0, 0, 0), (nb, 1, 0, 0), (own_up, 0, -1, 0), (own_down, 0, 1, 0), (far_a, 0, 2, 0), (far_b, 0, 2, 1),
                (nb_up, 1, -1, 0), (nb_down, 1, 1, 0), (nb_far_a, 1, 2, 0), (nb_far_b, 1, 2, 1)]
    right = [jnp.zeros((Z * half, columns), b_matrix.dtype) for _ in range(2)]
    for value, side, dy, sub in b_pieces:
        place = ((x_hi + side) % 2 * Y + (y + dy) % Y) * half + sub * (half // 2)
        right[0] = lax.dynamic_update_slice(right[0], value, (place, 0))
        right[1] = lax.dynamic_update_slice(right[1], moved(value, sibling), (place, 0))

    total = jnp.dot(left[0], right[0], preferred_element_type=jnp.float32)
    total = total + jnp.dot(left[1], right[1], preferred_element_type=jnp.float32)
    share = columns // 2
    away = lax.dynamic_slice(total, (0, (1 - x_lo) * share), (rows, share)).astype(jnp.bfloat16)
    keep = lax.dynamic_slice(total, (0, x_lo * share), (rows, share))
    return (keep + moved(away, x_pair).astype(jnp.float32)).astype(jnp.bfloat16)


def solution(mesh):
    in_specs = (P("col", "row"), P("col", "row"))
    out_specs = P("col", ("row", "depth"))
    return jax.shard_map(body, mesh=mesh, in_specs=in_specs, out_specs=out_specs, check_vma=False)
```

time: 554 us -> 144 us (0.26)
  waiting for transfers between devices: 360 us -> 68.3 us
  starting transfers between devices: 119 us -> 34.4 us
  matrix products: 35.5 us -> 11 us
  between operations: 13.5 us -> 0.68 us
  local copies, waits for them, and re-layouts: 15.4 us -> 24.2 us
  other arithmetic: 9.79 us -> 3.42 us
    ppermute x21 -> x27, waiting for transfers between devices: 318 us -> 68.3 us  [moved(): return lax.ppermute(value, AXES, pairs)]
    ppermute x21 -> x27, starting transfers between devices: 119 us -> 34.4 us  [moved(): return lax.ppermute(value, AXES, pairs)]
    unnamed x2 -> x0, waiting for transfers between devices: 42.1 us -> none
    dot_general x8 -> x2, matrix products: 35.5 us -> 11 us  [the longest x1 7.03 us: body(): total = jnp.dot(left[0], right[0], preferred_element_type=jnp.float32)]
    dynamic_update_slice x0 -> x29, local copies, waits for them, and re-layouts: none -> 15.1 us  [the longest x10 11.9 us: body(): right[0] = lax.dynamic_update_slice(right[0], value, (place, 0))]
    while x14 -> x0, local copies, waits for them, and re-layouts: 10.7 us -> none
    select_n x7 -> x0, other arithmetic: 9.31 us -> none  [the longest x4 8.02 us: body(): b_layer = jnp.where(b_offset // (1 << bit_index) % 2 == 1, shifted, b_layer)]
  transfers between devices with their start and end apart: 22 -> 27, of which waited for: 21 -> 7; matrix products, arithmetic and copies ran while one was open for 6% -> 19% of each run, Pallas kernels for 0% -> 0%
where the time goes in v1:
time: 144 us; the launch traced here: 142 us
  waiting for transfers between devices  68.3 us (47%)
  starting transfers between devices  34.4 us (24%)
  local copies, waits for them, and re-layouts  24.2 us (17%)
  matrix products  11 us (8%)
  other arithmetic  3.42 us (2%)
    ppermute x27, waiting for transfers between devices, moved(): return lax.ppermute(value, AXES, pairs)  68.3 us
    ppermute x27, starting transfers between devices, moved(): return lax.ppermute(value, AXES, pairs)  34.4 us
    dynamic_update_slice x10, local copies, waits for them, and re-layouts, body(): right[0] = lax.dynamic_update_slice(right[0], value, (place, 0))  11.9 us
    dot_general x1, matrix products, body(): total = jnp.dot(left[0], right[0], preferred_element_type=jnp.float32)  7.03 us
    another operation x4, local copies, waits for them, and re-layouts  4.35 us
    dot_general x1, matrix products, body(): jnp.dot(left[1], right[1], preferred_element_type=jnp.float32)  3.97 us
    unnamed x5, local copies, waits for them, and re-layouts  3.26 us
  transfers between devices with their start and end apart: 27, of which 7 were waited for; matrix products, arithmetic and copies ran while one was open for 19% of the time, Pallas kernels for 0%

profile of v1, /device:TPU:1, one launch (start us, length us, event | category | flops | bytes accessed | tf_op | source)
XLA Modules:
  0.0 142.0 jit_solution(3795152432484851240)
XLA Ops:
  0.0 1.5 %copy.3 = bf16[512,1024]{0,1:T(8,128)(2,1)S(1)} copy(bf16[512,1024]{1,0:T(8,128)(2,1)} %param.2) | data formatting | bytes 2097152 | tf_op args[0]
  1.9 0.8 pad_maximum_fusion
  2.7 2.5 %collective-permute-start = (bf16[512,512]{1,0:T(8,128)(2,1)}, bf16[512,512]{1,0:T(8,128)(2,1)}, u32[]{:S(2)}, u32[]{:S(2)}) collective-permute-start(bf16[512,512]{1,0:T(8,128)(2,1)} %pad_maximum_fusion), channel_id=1, source_target_pairs={{0,32},{1,33},{2,34},{3,35},{4,36},{5,37},{6,38},{7,39},{8,40},{9,... | collective-permute-start | bytes 1572872 | tf_op jit(solution)/shard_map/ppermute | solution.py:18
  5.2 3.9 %collective-permute-start.1 = (bf16[512,512]{1,0:T(8,128)(2,1)}, bf16[512,512]{1,0:T(8,128)(2,1)}, u32[]{:S(2)}, u32[]{:S(2)}) collective-permute-start(bf16[512,512]{1,0:T(8,128)(2,1)} %pad_maximum_fusion), channel_id=1, source_target_pairs={{0,224},{1,225},{2,226},{3,227},{4,228},{5,229},{6,230},{7,231},{8... | collective-permute-start | bytes 1572872 | tf_op jit(solution)/shard_map/ppermute | solution.py:18
  9.1 3.4 %broadcast.25.clone = bf16[2048,1792]{1,0:T(8,128)(2,1)} broadcast(bf16[]{:T(256)} %constant.152.clone.1), dimensions={} | broadcast | bytes 7340034 | tf_op jit(solution)/shard_map/broadcast.2
  12.5 1.4 constant_dynamic-update-slice_fusion.20
  13.8 2.5 %collective-permute-start.7 = (bf16[256,1792]{1,0:T(8,128)(2,1)}, bf16[256,1792]{1,0:T(8,128)(2,1)}, u32[]{:S(2)}, u32[]{:S(2)}) collective-permute-start(bf16[256,1792]{1,0:T(8,128)(2,1)} %get-tuple-element.6), channel_id=1, source_target_pairs={{0,17},{1,16},{2,19},{3,18},{4,21},{5,20},{6,23},{7,22},{8,25},{9,... | collective-permute-start | bytes 2752520 | tf_op jit(solution)/shard_map/ppermute | solution.py:18
  16.3 1.3 collective-permute-start.8
  17.6 1.4 collective-permute-start.9
  19.0 0.2 broadcast.24.clone
  19.6 0.2 broadcast.24.clone.1
  19.9 1.2 collective-permute-done
  21.1 1.2 collective-permute-start.16
  22.3 1.1 slice_dynamic-update-slice_fusion.6
  23.5 1.1 slice_dynamic-update-slice_fusion.5
  24.6 14.0 %collective-permute-done.8 = bf16[256,1792]{1,0:T(8,128)(2,1)} collective-permute-done((bf16[256,1792]{1,0:T(8,128)(2,1)}, bf16[256,1792]{1,0:T(8,128)(2,1)}, u32[]{:S(2)}, u32[]{:S(2)}) %collective-permute-start.8) | collective-permute-done | bytes 917536 | tf_op jit(solution)/shard_map/ppermute | solution.py:18
  38.6 1.2 collective-permute-start.3
  39.8 1.0 slice.71
  41.0 2.7 %collective-permute-start.11 = (bf16[128,1792]{1,0:T(8,128)(2,1)S(1)}, bf16[128,1792]{1,0:T(8,128)(2,1)S(1)}, u32[]{:S(2)}, u32[]{:S(2)}) collective-permute-start(bf16[128,1792]{1,0:T(8,128)(2,1)S(1)} %slice.72), channel_id=1, source_target_pairs={{0,12},{1,13},{2,14},{3,15},{4,0},{5,1},{6,2},{7,3},{8,4},{9,5},{1... | collective-permute-start | bytes 1376264 | tf_op jit(solution)/shard_map/ppermute | solution.py:18
  43.7 2.2 %constant_dynamic-update-slice_fusion.19 = bf16[2048,1792]{1,0:T(8,128)(2,1)} fusion(bf16[2048,1792]{1,0:T(8,128)(2,1)} %get-tuple-element.5, bf16[256,1792]{1,0:T(8,128)(2,1)} %collective-permute-done.7, s32[]{:T(128)S(6)} %select_n.221), kind=kLoop, calls=%fused_computation.37 | loop fusion | bytes 1835012 | tf_op jit(solution)/shard_map/dynamic_update_slice | solution.py:92
  45.9 2.2 %constant_dynamic-update-slice_fusion.18 = bf16[2048,1792]{1,0:T(8,128)(2,1)} fusion(bf16[2048,1792]{1,0:T(8,128)(2,1)} %constant_dynamic-update-slice_fusion.19, bf16[256,1792]{1,0:T(8,128)(2,1)} %collective-permute-done.8, s32[]{:T(128)S(6)} %select_n.223), kind=kLoop, calls=%fused_computation.36 | loop fusion | bytes 1835012 | tf_op jit(solution)/shard_map/dynamic_update_slice | solution.py:92
  48.1 1.0 constant_dynamic-update-slice_fusion.17
  49.1 0.5 broadcast.25
  49.7 3.3 %collective-permute-start.17 = (bf16[256,1792]{1,0:T(8,128)(2,1)}, bf16[256,1792]{1,0:T(8,128)(2,1)S(1)}, u32[]{:S(2)}, u32[]{:S(2)}) collective-permute-start(bf16[256,1792]{1,0:T(8,128)(2,1)} %collective-permute-done.7), channel_id=1, source_target_pairs={{0,2},{1,3},{2,0},{3,1},{4,6},{5,7},{6,4},{7,5},{8,10},{9,11},{10,... | collective-permute-start | bytes 2752520 | tf_op jit(solution)/shard_map/ppermute | solution.py:18
  53.0 0.3 collective-permute-start.4
  53.4 2.7 %collective-permute-start.5 = (bf16[512,512]{1,0:T(8,128)(2,1)S(1)}, bf16[512,512]{1,0:T(8,128)(2,1)S(1)}, u32[]{:S(2)}, u32[]{:S(2)}) collective-permute-start(bf16[512,512]{1,0:T(8,128)(2,1)S(1)} %collective-permute-done.3), channel_id=1, source_target_pairs={{0,224},{1,225},{2,226},{3,227},{4,228},{5,229},{6,230},{7,231},{8... | collective-permute-start | bytes 1572872 | tf_op jit(solution)/shard_map/ppermute | solution.py:18
  56.1 0.8 constant_dynamic-update-slice_fusion.16
  56.9 1.4 collective-permute-start.18
  58.3 0.8 constant_dynamic-update-slice_fusion.15
  59.1 8.9 %collective-permute-done.4 = bf16[512,512]{1,0:T(8,128)(2,1)S(1)} collective-permute-done((bf16[512,512]{1,0:T(8,128)(2,1)S(1)}, bf16[512,512]{1,0:T(8,128)(2,1)S(1)}, u32[]{:S(2)}, u32[]{:S(2)}) %collective-permute-start.4) | collective-permute-done | bytes 524320 | tf_op jit(solution)/shard_map/ppermute | solution.py:18
  68.0 0.8 collective-permute-start.19
  68.9 3.0 %collective-permute-start.13 = (bf16[256,1792]{1,0:T(8,128)(2,1)}, bf16[256,1792]{1,0:T(8,128)(2,1)S(1)}, u32[]{:S(2)}, u32[]{:S(2)}) collective-permute-start(bf16[256,1792]{1,0:T(8,128)(2,1)} %collective-permute-done.7), channel_id=1, source_target_pairs={{0,12},{1,13},{2,14},{3,15},{4,0},{5,1},{6,2},{7,3},{8,4},{9,5},{1... | collective-permute-start | bytes 2752520 | tf_op jit(solution)/shard_map/ppermute | solution.py:18
  72.0 0.3 collective-permute-start.14
  72.4 2.5 %collective-permute-start.15 = (bf16[128,1792]{1,0:T(8,128)(2,1)S(1)}, bf16[128,1792]{1,0:T(8,128)(2,1)S(1)}, u32[]{:S(2)}, u32[]{:S(2)}) collective-permute-start(bf16[128,1792]{1,0:T(8,128)(2,1)S(1)} %collective-permute-done.11), channel_id=1, source_target_pairs={{0,17},{1,16},{2,19},{3,18},{4,21},{5,20},{6,23},{7,22},{8,25},{9,... | collective-permute-start | bytes 1376264 | tf_op jit(solution)/shard_map/ppermute | solution.py:18
  75.1 0.9 collective-permute-start.20
  76.2 1.0 constant_dynamic-update-slice_fusion.14
  77.2 14.9 %collective-permute-done.13 = bf16[256,1792]{1,0:T(8,128)(2,1)S(1)} collective-permute-done((bf16[256,1792]{1,0:T(8,128)(2,1)}, bf16[256,1792]{1,0:T(8,128)(2,1)S(1)}, u32[]{:S(2)}, u32[]{:S(2)}) %collective-permute-start.13) | collective-permute-done | bytes 917536 | tf_op jit(solution)/shard_map/ppermute | solution.py:18
  92.0 1.0 constant_dynamic-update-slice_fusion.13
  93.1 0.8 collective-permute-start.22
  94.0 0.8 constant_dynamic-update-slice_fusion.12
  95.0 1.1 collective-permute-start.24
  96.1 0.8 constant_dynamic-update-slice_fusion.11
  96.9 9.0 %collective-permute-done.6 = bf16[512,512]{1,0:T(8,128)(2,1)S(1)} collective-permute-done((bf16[512,512]{1,0:T(8,128)(2,1)S(1)}, bf16[512,512]{1,0:T(8,128)(2,1)S(1)}, u32[]{:S(2)}, u32[]{:S(2)}) %collective-permute-start.6) | collective-permute-done | bytes 524320 | tf_op jit(solution)/shard_map/ppermute | solution.py:18
  106.0 7.0 %fusion = f32[512,1792]{1,0:T(8,128)S(1)} fusion(bf16[512,2048]{1,0:T(8,128)(2,1)S(1)} %get-tuple-element.10, bf16[2048,1792]{1,0:T(8,128)(2,1)} %constant_dynamic-update-slice_fusion.11), kind=kOutput, calls=%fused_computation.43 | convolution fusion | flops 3758096384 | bytes 13107200 | tf_op jit(solution)/shard_map/dot_general | solution.py:95
  113.3 4.0 %convolution_add_fusion = f32[512,1792]{1,0:T(8,128)S(1)} fusion(f32[512,1792]{1,0:T(8,128)S(1)} %fusion, bf16[512,2048]{1,0:T(8,128)(2,1)S(1)} %get-tuple-element.9, bf16[2048,1792]{1,0:T(8,128)(2,1)S(1)} %constant_dynamic-update-slice_fusion), kind=kOutput, calls=%fused_computation | convolution fusion | flops 3759013888 | bytes 16777216 | tf_op jit(solution)/shard_map/dot_general | solution.py:96
  117.3 1.8 %copy-done = f32[512,1792]{1,0:T(8,128)} copy-done((f32[512,1792]{1,0:T(8,128)}, f32[512,1792]{1,0:T(8,128)S(1)}, u32[]{:S(2)}) %copy-start) | copy-done | bytes 3670040
  119.3 20.2 %collective-permute-done.26 = bf16[512,896]{1,0:T(8,128)(2,1)S(1)} collective-permute-done((bf16[512,896]{1,0:T(8,128)(2,1)S(1)}, bf16[512,896]{1,0:T(8,128)(2,1)S(1)}, u32[]{:S(2)}, u32[]{:S(2)}) %collective-permute-start.26) | collective-permute-done | bytes 917536 | tf_op jit(solution)/shard_map/ppermute | solution.py:18
  139.5 2.6 %add_convert_fusion = bf16[512,896]{1,0:T(8,128)(2,1)} fusion(bf16[512,896]{1,0:T(8,128)(2,1)S(1)} %collective-permute-done.26, f32[512,1792]{1,0:T(8,128)} %copy-done, s32[]{:T(128)S(6)} %select_n.233), kind=kLoop, calls=%fused_computation.1 | loop fusion | flops 1376256 | bytes 3670020 | tf_op jit(solution)/shard_map/convert_element_type | solution.py:100
  (54 shorter events, 2.1 us)
Async XLA Ops:
  2.7 18.4 %collective-permute-start = (bf16[512,512]{1,0:T(8,128)(2,1)}, bf16[512,512]{1,0:T(8,128)(2,1)}, u32[]{:S(2)}, u32[]{:S(2)}) collective-permute-start(bf16[512,512]{1,0:T(8,128)(2,1)} %pad_maximum_fusion), channel_id=1, source_target_pairs={{0,32},{1,33},{2,34},{3,35},{4,36},{5,37},{6,38},{7,39},{8,40},{9,... | collective-permute-start | bytes 1572872 | tf_op jit(solution)/shard_map/ppermute | solution.py:18
  5.2 18.2 %collective-permute-start.1 = (bf16[512,512]{1,0:T(8,128)(2,1)}, bf16[512,512]{1,0:T(8,128)(2,1)}, u32[]{:S(2)}, u32[]{:S(2)}) collective-permute-start(bf16[512,512]{1,0:T(8,128)(2,1)} %pad_maximum_fusion), channel_id=1, source_target_pairs={{0,224},{1,225},{2,226},{3,227},{4,228},{5,229},{6,230},{7,231},{8... | collective-permute-start | bytes 1572872 | tf_op jit(solution)/shard_map/ppermute | solution.py:18
  9.1 3.4 %copy-start.1 = (bf16[512,1792]{1,0:T(8,128)(2,1)S(1)}, bf16[512,1792]{1,0:T(8,128)(2,1)}, u32[]{:S(2)}) copy-start(bf16[512,1792]{1,0:T(8,128)(2,1)} %param.3) | copy-start | bytes 5505028
  13.8 27.1 %collective-permute-start.7 = (bf16[256,1792]{1,0:T(8,128)(2,1)}, bf16[256,1792]{1,0:T(8,128)(2,1)}, u32[]{:S(2)}, u32[]{:S(2)}) collective-permute-start(bf16[256,1792]{1,0:T(8,128)(2,1)} %get-tuple-element.6), channel_id=1, source_target_pairs={{0,17},{1,16},{2,19},{3,18},{4,21},{5,20},{6,23},{7,22},{8,25},{9,... | collective-permute-start | bytes 2752520 | tf_op jit(solution)/shard_map/ppermute | solution.py:18
  16.3 22.3 %collective-permute-start.8 = (bf16[256,1792]{1,0:T(8,128)(2,1)}, bf16[256,1792]{1,0:T(8,128)(2,1)}, u32[]{:S(2)}, u32[]{:S(2)}) collective-permute-start(bf16[256,1792]{1,0:T(8,128)(2,1)} %get-tuple-element.6), channel_id=1, source_target_pairs={{0,4},{1,5},{2,6},{3,7},{4,8},{5,9},{6,10},{7,11},{8,12},{9,13},{1... | collective-permute-start | bytes 2752520 | tf_op jit(solution)/shard_map/ppermute | solution.py:18
  17.6 23.2 %collective-permute-start.9 = (bf16[256,1792]{1,0:T(8,128)(2,1)}, bf16[256,1792]{1,0:T(8,128)(2,1)S(1)}, u32[]{:S(2)}, u32[]{:S(2)}) collective-permute-start(bf16[256,1792]{1,0:T(8,128)(2,1)} %get-tuple-element.6), channel_id=1, source_target_pairs={{0,12},{1,13},{2,14},{3,15},{4,0},{5,1},{6,2},{7,3},{8,4},{9,5},{1... | collective-permute-start | bytes 2752520 | tf_op jit(solution)/shard_map/ppermute | solution.py:18
  21.1 28.0 %collective-permute-start.16 = (bf16[256,1792]{1,0:T(8,128)(2,1)}, bf16[256,1792]{1,0:T(8,128)(2,1)S(1)}, u32[]{:S(2)}, u32[]{:S(2)}) collective-permute-start(bf16[256,1792]{1,0:T(8,128)(2,1)} %get-tuple-element.6), channel_id=1, source_target_pairs={{0,2},{1,3},{2,0},{3,1},{4,6},{5,7},{6,4},{7,5},{8,10},{9,11},{10,... | collective-permute-start | bytes 2752520 | tf_op jit(solution)/shard_map/ppermute | solution.py:18
  23.4 26.3 %collective-permute-start.2 = (bf16[512,512]{1,0:T(8,128)(2,1)}, bf16[512,512]{1,0:T(8,128)(2,1)S(1)}, u32[]{:S(2)}, u32[]{:S(2)}) collective-permute-start(bf16[512,512]{1,0:T(8,128)(2,1)} %collective-permute-done), channel_id=1, source_target_pairs={{0,32},{1,33},{2,34},{3,35},{4,36},{5,37},{6,38},{7,39},{8,40},{9,... | collective-permute-start | bytes 1572872 | tf_op jit(solution)/shard_map/ppermute | solution.py:18
  38.6 14.4 %collective-permute-start.3 = (bf16[512,512]{1,0:T(8,128)(2,1)}, bf16[512,512]{1,0:T(8,128)(2,1)S(1)}, u32[]{:S(2)}, u32[]{:S(2)}) collective-permute-start(bf16[512,512]{1,0:T(8,128)(2,1)} %collective-permute-done.1), channel_id=1, source_target_pairs={{0,224},{1,225},{2,226},{3,227},{4,228},{5,229},{6,230},{7,231},{8... | collective-permute-start | bytes 1572872 | tf_op jit(solution)/shard_map/ppermute | solution.py:18
  40.9 12.5 %collective-permute-start.10 = (bf16[128,1792]{1,0:T(8,128)(2,1)S(1)}, bf16[128,1792]{1,0:T(8,128)(2,1)S(1)}, u32[]{:S(2)}, u32[]{:S(2)}) collective-permute-start(bf16[128,1792]{1,0:T(8,128)(2,1)S(1)} %slice.71), channel_id=1, source_target_pairs={{0,4},{1,5},{2,6},{3,7},{4,8},{5,9},{6,10},{7,11},{8,12},{9,13},{1... | collective-permute-start | bytes 1376264 | tf_op jit(solution)/shard_map/ppermute | solution.py:18
  41.0 15.9 %collective-permute-start.11 = (bf16[128,1792]{1,0:T(8,128)(2,1)S(1)}, bf16[128,1792]{1,0:T(8,128)(2,1)S(1)}, u32[]{:S(2)}, u32[]{:S(2)}) collective-permute-start(bf16[128,1792]{1,0:T(8,128)(2,1)S(1)} %slice.72), channel_id=1, source_target_pairs={{0,12},{1,13},{2,14},{3,15},{4,0},{5,1},{6,2},{7,3},{8,4},{9,5},{1... | collective-permute-start | bytes 1376264 | tf_op jit(solution)/shard_map/ppermute | solution.py:18
  49.1 27.0 %collective-permute-start.12 = (bf16[256,1792]{1,0:T(8,128)(2,1)}, bf16[256,1792]{1,0:T(8,128)(2,1)S(1)}, u32[]{:S(2)}, u32[]{:S(2)}) collective-permute-start(bf16[256,1792]{1,0:T(8,128)(2,1)} %collective-permute-done.7), channel_id=1, source_target_pairs={{0,4},{1,5},{2,6},{3,7},{4,8},{5,9},{6,10},{7,11},{8,12},{9,13},{1... | collective-permute-start | bytes 2752520 | tf_op jit(solution)/shard_map/ppermute | solution.py:18
  49.7 22.4 %collective-permute-start.17 = (bf16[256,1792]{1,0:T(8,128)(2,1)}, bf16[256,1792]{1,0:T(8,128)(2,1)S(1)}, u32[]{:S(2)}, u32[]{:S(2)}) collective-permute-start(bf16[256,1792]{1,0:T(8,128)(2,1)} %collective-permute-done.7), channel_id=1, source_target_pairs={{0,2},{1,3},{2,0},{3,1},{4,6},{5,7},{6,4},{7,5},{8,10},{9,11},{10,... | collective-permute-start | bytes 2752520 | tf_op jit(solution)/shard_map/ppermute | solution.py:18
  53.0 15.0 %collective-permute-start.4 = (bf16[512,512]{1,0:T(8,128)(2,1)S(1)}, bf16[512,512]{1,0:T(8,128)(2,1)S(1)}, u32[]{:S(2)}, u32[]{:S(2)}) collective-permute-start(bf16[512,512]{1,0:T(8,128)(2,1)S(1)} %collective-permute-done.2), channel_id=1, source_target_pairs={{0,32},{1,33},{2,34},{3,35},{4,36},{5,37},{6,38},{7,39},{8,40},{9,... | collective-permute-start | bytes 1572872 | tf_op jit(solution)/shard_map/ppermute | solution.py:18
  53.4 15.5 %collective-permute-start.5 = (bf16[512,512]{1,0:T(8,128)(2,1)S(1)}, bf16[512,512]{1,0:T(8,128)(2,1)S(1)}, u32[]{:S(2)}, u32[]{:S(2)}) collective-permute-start(bf16[512,512]{1,0:T(8,128)(2,1)S(1)} %collective-permute-done.3), channel_id=1, source_target_pairs={{0,224},{1,225},{2,226},{3,227},{4,228},{5,229},{6,230},{7,231},{8... | collective-permute-start | bytes 1572872 | tf_op jit(solution)/shard_map/ppermute | solution.py:18
  56.9 15.5 %collective-permute-start.18 = (bf16[256,1792]{1,0:T(8,128)(2,1)}, bf16[256,1792]{1,0:T(8,128)(2,1)S(1)}, u32[]{:S(2)}, u32[]{:S(2)}) collective-permute-start(bf16[256,1792]{1,0:T(8,128)(2,1)} %collective-permute-done.8), channel_id=1, source_target_pairs={{0,2},{1,3},{2,0},{3,1},{4,6},{5,7},{6,4},{7,5},{8,10},{9,11},{10,... | collective-permute-start | bytes 2752520 | tf_op jit(solution)/shard_map/ppermute | solution.py:18
  68.0 7.0 %collective-permute-start.19 = (bf16[256,1792]{1,0:T(8,128)(2,1)S(1)}, bf16[256,1792]{1,0:T(8,128)(2,1)S(1)}, u32[]{:S(2)}, u32[]{:S(2)}) collective-permute-start(bf16[256,1792]{1,0:T(8,128)(2,1)S(1)} %collective-permute-done.9), channel_id=1, source_target_pairs={{0,2},{1,3},{2,0},{3,1},{4,6},{5,7},{6,4},{7,5},{8,10},{9,11},{10,... | collective-permute-start | bytes 2752520 | tf_op jit(solution)/shard_map/ppermute | solution.py:18
  68.9 23.1 %collective-permute-start.13 = (bf16[256,1792]{1,0:T(8,128)(2,1)}, bf16[256,1792]{1,0:T(8,128)(2,1)S(1)}, u32[]{:S(2)}, u32[]{:S(2)}) collective-permute-start(bf16[256,1792]{1,0:T(8,128)(2,1)} %collective-permute-done.7), channel_id=1, source_target_pairs={{0,12},{1,13},{2,14},{3,15},{4,0},{5,1},{6,2},{7,3},{8,4},{9,5},{1... | collective-permute-start | bytes 2752520 | tf_op jit(solution)/shard_map/ppermute | solution.py:18
  72.0 21.9 %collective-permute-start.14 = (bf16[128,1792]{1,0:T(8,128)(2,1)S(1)}, bf16[128,1792]{1,0:T(8,128)(2,1)S(1)}, u32[]{:S(2)}, u32[]{:S(2)}) collective-permute-start(bf16[128,1792]{1,0:T(8,128)(2,1)S(1)} %collective-permute-done.10), channel_id=1, source_target_pairs={{0,17},{1,16},{2,19},{3,18},{4,21},{5,20},{6,23},{7,22},{8,25},{9,... | collective-permute-start | bytes 1376264 | tf_op jit(solution)/shard_map/ppermute | solution.py:18
  72.4 22.6 %collective-permute-start.15 = (bf16[128,1792]{1,0:T(8,128)(2,1)S(1)}, bf16[128,1792]{1,0:T(8,128)(2,1)S(1)}, u32[]{:S(2)}, u32[]{:S(2)}) collective-permute-start(bf16[128,1792]{1,0:T(8,128)(2,1)S(1)} %collective-permute-done.11), channel_id=1, source_target_pairs={{0,17},{1,16},{2,19},{3,18},{4,21},{5,20},{6,23},{7,22},{8,25},{9,... | collective-permute-start | bytes 1376264 | tf_op jit(solution)/shard_map/ppermute | solution.py:18
  75.1 18.0 %collective-permute-start.20 = (bf16[128,1792]{1,0:T(8,128)(2,1)S(1)}, bf16[128,1792]{1,0:T(8,128)(2,1)S(1)}, u32[]{:S(2)}, u32[]{:S(2)}) collective-permute-start(bf16[128,1792]{1,0:T(8,128)(2,1)S(1)} %collective-permute-done.10), channel_id=1, source_target_pairs={{0,2},{1,3},{2,0},{3,1},{4,6},{5,7},{6,4},{7,5},{8,10},{9,11},{10,... | collective-permute-start | bytes 1376264 | tf_op jit(solution)/shard_map/ppermute | solution.py:18
  76.1 20.8 %collective-permute-start.21 = (bf16[128,1792]{1,0:T(8,128)(2,1)S(1)}, bf16[128,1792]{1,0:T(8,128)(2,1)S(1)}, u32[]{:S(2)}, u32[]{:S(2)}) collective-permute-start(bf16[128,1792]{1,0:T(8,128)(2,1)S(1)} %collective-permute-done.11), channel_id=1, source_target_pairs={{0,2},{1,3},{2,0},{3,1},{4,6},{5,7},{6,4},{7,5},{8,10},{9,11},{10,... | collective-permute-start | bytes 1376264 | tf_op jit(solution)/shard_map/ppermute | solution.py:18
  92.0 13.9 %collective-permute-start.6 = (bf16[512,512]{1,0:T(8,128)(2,1)S(1)}, bf16[512,512]{1,0:T(8,128)(2,1)S(1)}, u32[]{:S(2)}, u32[]{:S(2)}) collective-permute-start(bf16[512,512]{1,0:T(8,128)(2,1)S(1)} %collective-permute-done.4), channel_id=1, source_target_pairs={{0,32},{1,33},{2,34},{3,35},{4,36},{5,37},{6,38},{7,39},{8,40},{9,... | collective-permute-start | bytes 1572872 | tf_op jit(solution)/shard_map/ppermute | solution.py:18
  93.1 20.0 %collective-permute-start.22 = (bf16[256,1792]{1,0:T(8,128)(2,1)S(1)}, bf16[256,1792]{1,0:T(8,128)(2,1)S(1)}, u32[]{:S(2)}, u32[]{:S(2)}) collective-permute-start(bf16[256,1792]{1,0:T(8,128)(2,1)S(1)} %collective-permute-done.12), channel_id=1, source_target_pairs={{0,2},{1,3},{2,0},{3,1},{4,6},{5,7},{6,4},{7,5},{8,10},{9,11},{10,... | collective-permute-start | bytes 2752520 | tf_op jit(solution)/shard_map/ppermute | solution.py:18
  93.9 19.2 %collective-permute-start.23 = (bf16[256,1792]{1,0:T(8,128)(2,1)S(1)}, bf16[256,1792]{1,0:T(8,128)(2,1)S(1)}, u32[]{:S(2)}, u32[]{:S(2)}) collective-permute-start(bf16[256,1792]{1,0:T(8,128)(2,1)S(1)} %collective-permute-done.13), channel_id=1, source_target_pairs={{0,2},{1,3},{2,0},{3,1},{4,6},{5,7},{6,4},{7,5},{8,10},{9,11},{10,... | collective-permute-start | bytes 2752520 | tf_op jit(solution)/shard_map/ppermute | solution.py:18
  95.0 18.2 %collective-permute-start.24 = (bf16[128,1792]{1,0:T(8,128)(2,1)S(1)}, bf16[128,1792]{1,0:T(8,128)(2,1)S(1)}, u32[]{:S(2)}, u32[]{:S(2)}) collective-permute-start(bf16[128,1792]{1,0:T(8,128)(2,1)S(1)} %collective-permute-done.14), channel_id=1, source_target_pairs={{0,2},{1,3},{2,0},{3,1},{4,6},{5,7},{6,4},{7,5},{8,10},{9,11},{10,... | collective-permute-start | bytes 1376264 | tf_op jit(solution)/shard_map/ppermute | solution.py:18
  96.9 16.4 %collective-permute-start.25 = (bf16[128,1792]{1,0:T(8,128)(2,1)S(1)}, bf16[128,1792]{1,0:T(8,128)(2,1)S(1)}, u32[]{:S(2)}, u32[]{:S(2)}) collective-permute-start(bf16[128,1792]{1,0:T(8,128)(2,1)S(1)} %collective-permute-done.15), channel_id=1, source_target_pairs={{0,2},{1,3},{2,0},{3,1},{4,6},{5,7},{6,4},{7,5},{8,10},{9,11},{10,... | collective-permute-start | bytes 1376264 | tf_op jit(solution)/shard_map/ppermute | solution.py:18
  117.3 1.8 %copy-start = (f32[512,1792]{1,0:T(8,128)}, f32[512,1792]{1,0:T(8,128)S(1)}, u32[]{:S(2)}) copy-start(f32[512,1792]{1,0:T(8,128)S(1)} %convolution_add_fusion) | copy-start | bytes 11010052
  119.2 20.3 %collective-permute-start.26 = (bf16[512,896]{1,0:T(8,128)(2,1)S(1)}, bf16[512,896]{1,0:T(8,128)(2,1)S(1)}, u32[]{:S(2)}, u32[]{:S(2)}) collective-permute-start(bf16[512,896]{1,0:T(8,128)(2,1)S(1)} %dynamic-slice_convert_fusion), channel_id=1, source_target_pairs={{0,1},{1,0},{2,3},{3,2},{4,5},{5,4},{6,7},{7,6},{8,9},{9,8},{10,11... | collective-permute-start | bytes 2752520 | tf_op jit(solution)/shard_map/ppermute | solution.py:18

commit v2 on v1

v2 whole, which is shorter than its diff:
```python
import functools

import jax
import jax.numpy as jnp
from jax import lax
from jax.experimental import pallas as pl
from jax.experimental.pallas import tpu as pltpu
from jax.sharding import PartitionSpec as P

AXES = ("row", "col", "depth")
Z, X, Y = 8, 2, 4
TILE = 256


def moved(value, target):
    def number(z, x_hi, y, core, x_lo):
        return (((z * X + x_hi) * Y + y) * 2 + core) * 2 + x_lo

    pairs = [
        (number(z, x_hi, y, core, x_lo), number(*target(z, x_hi, y, core, x_lo)))
        for z in range(Z)
        for x_hi in range(X)
        for y in range(Y)
        for core in range(2)
        for x_lo in range(2)
    ]
    return lax.ppermute(value, AXES, pairs)


def z_up(z, x_hi, y, core, x_lo):
    return (z + 1) % Z, x_hi, y, core, x_lo


def z_down(z, x_hi, y, core, x_lo):
    return (z - 1) % Z, x_hi, y, core, x_lo


def y_up(z, x_hi, y, core, x_lo):
    return z, x_hi, (y + 1) % Y, core, x_lo


def y_down(z, x_hi, y, core, x_lo):
    return z, x_hi, (y - 1) % Y, core, x_lo


def x_side(z, x_hi, y, core, x_lo):
    return z, 1 - x_hi, y, core, 1 - x_lo


def x_pair(z, x_hi, y, core, x_lo):
    return z, x_hi, y, core, 1 - x_lo


def sibling(z, x_hi, y, core, x_lo):
    return z, x_hi, y, 1 - core, x_lo


def pack_kernel(places, *refs):
    pieces, packed, sem = refs[:len(places)], refs[-2], refs[-1]
    rows = packed.shape[1] // 2
    z = lax.axis_index("row")
    copies = []
    for index, (block, offset) in enumerate(places):
        place = packed.at[lax.rem(z + offset, Z), pl.ds(block * rows, pieces[index].shape[0])]
        copies.append(pltpu.make_async_copy(pieces[index], place, sem.at[index]))
    for copy in copies:
        copy.start()
    for copy in copies:
        copy.wait()


def packed_left(pieces, rows):
    values, places = zip(*pieces)
    half = values[0].shape[1]
    return pl.pallas_call(
        functools.partial(pack_kernel, places),
        out_shape=jax.ShapeDtypeStruct((Z, 2 * rows, half), jnp.bfloat16),
        in_specs=[pl.BlockSpec(memory_space=pl.ANY)] * len(values),
        out_specs=pl.BlockSpec(memory_space=pltpu.VMEM),
        scratch_shapes=[pltpu.SemaphoreType.DMA((len(values),))],
        compiler_params=pltpu.CompilerParams(vmem_limit_bytes=12 * 1024 * 1024),
        cost_estimate=pl.CostEstimate(flops=0, bytes_accessed=8 * Z * rows * half, transcendentals=0),
    )(*values)


def product_kernel(places, left, *refs):
    rights = refs[:len(places)]
    keep, send, total = refs[len(places):]
    _, rows, share = keep.shape
    col = lax.axis_index("col")
    x_lo = lax.axis_index("depth")
    x_hi, y = col // (2 * Y), col // 2 % Y
    for block in (1, 0):
        for index, (side, dy, first) in enumerate(places):
            place = lax.rem(x_hi + side, X) * Y + lax.rem(y + dy, Y)
            term = jnp.dot(
                left[place, block * rows:(block + 1) * rows],
                rights[index][:, first:first + 2 * share],
                preferred_element_type=jnp.float32,
            )
            total[...] = total[...] + term if index else term
        for d in range(2):
            target = send if block else keep
            target[lax.rem(x_lo + d, 2)] = total[:, d * share:(d + 1) * share].astype(target.dtype)


def product(left, pieces, columns):
    values, places = zip(*pieces)
    rows, inner = left.shape[1] // 2, left.shape[0] * left.shape[2]
    vmem = pl.BlockSpec(memory_space=pltpu.VMEM)
    return pl.pallas_call(
        functools.partial(product_kernel, places),
        out_shape=(
            jax.ShapeDtypeStruct((2, rows, columns // 2), jnp.float32),
            jax.ShapeDtypeStruct((2, rows, columns // 2), jnp.bfloat16),
        ),
        in_specs=[vmem] * (1 + len(values)),
        out_specs=(vmem, vmem),
        scratch_shapes=[pltpu.VMEM((rows, columns), jnp.float32)],
        compiler_params=pltpu.CompilerParams(vmem_limit_bytes=24 * 1024 * 1024),
        cost_estimate=pl.CostEstimate(
            flops=4 * rows * inner * columns, bytes_accessed=4 * inner * (rows + columns), transcendentals=0
        ),
    )(left, *values)


class Held:
    def __init__(self, **values):
        self.values = dict(values)

    def gate(self, *names):
        names = list(dict.fromkeys(names))
        if len(names) > 1:
            for name, value in zip(names, lax.optimization_barrier([self.values[n] for n in names]), strict=True):
                self.values[name] = value

    def move(self, name, source, target, after=()):
        self.gate(source, *after)
        self.values[name] = moved(self.values[source], target)


def body(a_matrix, b_matrix):
    rows = a_matrix.shape[0]
    depth, columns = b_matrix.shape
    half = depth // 2
    share = columns // 2
    col = lax.axis_index("col")
    x_lo = lax.axis_index("depth")
    x_hi, core = col // (2 * Y), col % 2
    part = x_hi ^ x_lo
    wide = -(-share // (2 * TILE)) * TILE

    def cut(first, width):
        return jnp.concatenate(
            [lax.dynamic_slice(b_matrix, (part * half, d * share + first), (half, width)) for d in range(2)], 1
        )

    other = lax.dynamic_slice(a_matrix, (0, (1 - core) * depth + part * half), (rows, half))
    mine = lax.dynamic_slice(a_matrix, (0, core * depth + part * half), (rows, half))
    held = Held(o=jnp.concatenate([cut(0, wide), cut(wide, share - wide)], 1))
    values, move, gate = held.values, held.move, held.gate
    values["other"] = other
    move("sib", "other", sibling)
    gate("sib", "o")
    move("u", "o", y_up)
    move("d", "o", y_down)
    move("n", "o", x_side)
    values["p"] = jnp.concatenate([mine, values["sib"]], 0)
    move("u1", "p", z_up)
    move("d1", "p", z_down)

    gate("u1", "d1")
    move("u2", "u1", z_up)
    move("d2", "d1", z_down)

    gate("u", "d", "n")
    values["ua"], values["db"] = values["u"][:, :2 * wide], values["d"][:, 2 * wide:]
    move("fa", "ua", y_up)
    move("fb", "db", y_down)

    gate("u2", "d2", "u", "d", "n")
    move("u3", "u2", z_up)
    move("d3", "d2", z_down)

    gate("fa", "fb", "u2", "d2", "n")
    move("nu", "n", y_up)
    move("nd", "n", y_down)
    move("nfa", "fa", x_side)
    move("nfb", "fb", x_side)

    gate("u3", "d3")
    values["u3h"], values["d3h"] = values["u3"][:rows], values["d3"][rows:]
    move("u4", "u3h", z_up)
    move("d4", "d3h", z_down)

    a_pieces = [("p", 0, 0), ("u1", 0, Z - 1), ("d1", 0, 1), ("u2", 0, Z - 2), ("d2", 0, 2),
                ("u3", 0, Z - 3), ("d3", 0, 3), ("u4", 0, Z // 2), ("d4", 1, Z // 2)]
    gate("nfa", "u4")
    left = packed_left([(values[k], tuple(v)) for k, *v in a_pieces], rows)
    parts = []
    for chunk, first in (("b", 2 * wide), ("a", 0)):
        b_pieces = [("o", 0, 0, first), ("n", 1, 0, first), ("u", 0, Y - 1, first), ("d", 0, 1, first), ("f" + chunk, 0, 2, 0),
                    ("nu", 1, Y - 1, first), ("nd", 1, 1, first), ("nf" + chunk, 1, 2, 0)]
        keep, send = product(left, [(values[k], tuple(v)) for k, *v in b_pieces],
                             values["f" + chunk].shape[1])
        came = moved(send, sibling)
        left, _ = lax.optimization_barrier((left, send))
        away = (keep[1] + came[1].astype(jnp.float32)).astype(jnp.bfloat16)
        arrived = moved(away, x_pair)
        parts.append((keep[0] + came[0].astype(jnp.float32) + arrived.astype(jnp.float32)).astype(jnp.bfloat16))
    first = lax.pad(parts[0], jnp.zeros((), jnp.bfloat16), ((0, 0, 0), (wide, 0, 0)))
    return lax.dynamic_update_slice(first, parts[1], (0, 0))


def solution(mesh):
    in_specs = (P("col", "row"), P("col", "row"))
    out_specs = P("col", ("row", "depth"))
    return jax.shard_map(body, mesh=mesh, in_specs=in_specs, out_specs=out_specs, check_vma=False)
```

time: 144 us -> 103 us (0.72); the launches traced: 142 us -> 103 us
  local copies, waits for them, and re-layouts: 24.2 us -> 3.32 us
  matrix products: 11 us -> 0 us
  waiting for transfers between devices: 68.3 us -> 58.4 us
  Pallas kernels: 0 us -> 8.3 us
  starting transfers between devices: 34.4 us -> 30.9 us
  other arithmetic: 3.42 us -> 1.7 us
    dynamic_update_slice x29 -> x0, local copies, waits for them, and re-layouts: 15.1 us -> none  [the longest x10 11.9 us: body(): right[0] = lax.dynamic_update_slice(right[0], value, (place, 0))]
    dot_general x2 -> x0, matrix products: 11 us -> none  [the longest x1 7.03 us: body(): total = jnp.dot(left[0], right[0], preferred_element_type=jnp.float32)]
    ppermute x27 -> x22, waiting for transfers between devices: 68.3 us -> 58.4 us  [moved(): return lax.ppermute(value, AXES, pairs)]
    pallas_call x0 -> x3, Pallas kernels: none -> 8.3 us  [the longest x2 7.92 us: product(): pl.pallas_call(functools.partial(product_kernel, places), out_shape=(jax....]
    another operation x4 -> x0, local copies, waits for them, and re-layouts: 4.35 us -> none
    ppermute x27 -> x22, starting transfers between devices: 34.4 us -> 30.9 us  [moved(): return lax.ppermute(value, AXES, pairs)]
    unnamed x5 -> x0, local copies, waits for them, and re-layouts: 3.26 us -> none
    dynamic_slice x3, local copies, waits for them, and re-layouts: 0.31 us -> 3.2 us  [the longest x2 2.14 us: cut(): lax.dynamic_slice(b_matrix, (part * half, d * share + first), (half, width))]
  transfers between devices with their start and end apart: 27 -> 22, of which waited for: 7 -> 11; matrix products, arithmetic and copies ran while one was open for 19% -> 3% of each run, Pallas kernels for 0% -> 5%
where the time goes in v2:
time: 103 us
  waiting for transfers between devices  58.4 us (57%)
  starting transfers between devices  30.9 us (30%)
  Pallas kernels  8.3 us (8%)
  local copies, waits for them, and re-layouts  3.32 us (3%)
  other arithmetic  1.7 us (2%)
    ppermute x22, waiting for transfers between devices, moved(): return lax.ppermute(value, AXES, pairs)  58.4 us
    ppermute x22, starting transfers between devices, moved(): return lax.ppermute(value, AXES, pairs)  30.9 us
    pallas_call x2, Pallas kernels, product(): pl.pallas_call(functools.partial(product_kernel, places), out_shape=(jax....  7.92 us
    dynamic_slice x2, local copies, waits for them, and re-layouts, cut(): lax.dynamic_slice(b_matrix, (part * half, d * share + first), (half, width))  2.14 us
  transfers between devices with their start and end apart: 22, of which 11 were waited for; matrix products, arithmetic and copies ran while one was open for 3% of the time, Pallas kernels for 5%

profile of v2, /device:TPU:1, one launch (start us, length us, event | category | flops | bytes accessed | tf_op | source)
XLA Modules:
  0.0 102.8 jit_solution(14206519154064214661)
XLA Ops:
  0.0 1.1 %constant_dynamic-slice_fusion.2 = (bf16[512,256]{1,0:T(8,128)(2,1)S(1)}, bf16[512,256]{1,0:T(8,128)(2,1)S(1)}) fusion(bf16[512,1024]{1,0:T(8,128)(2,1)} %param.2, s32[]{:T(128)S(6)} %select_n.25, s32[]{:T(128)S(6)} %select_n.26), kind=kLoop, calls=%fused_computation.13 | loop fusion | bytes 1048584 | tf_op jit(solution)/shard_map/dynamic_slice | solution.py:159
  1.1 3.3 %collective-permute-start = (bf16[512,256]{1,0:T(8,128)(2,1)S(1)}, bf16[512,256]{1,0:T(8,128)(2,1)S(1)}, u32[]{:S(2)}, u32[]{:S(2)}) collective-permute-start(bf16[512,256]{1,0:T(8,128)(2,1)S(1)} %get-tuple-element.62), channel_id=1, source_target_pairs={{0,2},{1,3},{2,0},{3,1},{4,6},{5,7},{6,4},{7,5},{8,10},{9,11},{10,... | collective-permute-start | bytes 786440 | tf_op jit(solution)/shard_map/ppermute | solution.py:27
  4.4 1.1 %constant_dynamic-slice_fusion = (bf16[256,512]{1,0:T(8,128)(2,1)S(1)}, bf16[256,512]{1,0:T(8,128)(2,1)S(1)}) fusion(bf16[512,1792]{1,0:T(8,128)(2,1)} %param.3, s32[]{:T(128)S(6)} %select_n.27), kind=kLoop, calls=%fused_computation.11 | loop fusion | bytes 1048580 | tf_op jit(solution)/shard_map/dynamic_slice | solution.py:155
  5.5 1.1 %constant_dynamic-slice_fusion.5 = (bf16[256,384]{1,0:T(8,128)(2,1)S(1)}, bf16[256,384]{1,0:T(8,128)(2,1)S(1)}) fusion(bf16[512,1792]{1,0:T(8,128)(2,1)} %param.3, s32[]{:T(128)S(6)} %select_n.27), kind=kLoop, calls=%fused_computation.16 | loop fusion | bytes 786436 | tf_op jit(solution)/shard_map/dynamic_slice | solution.py:155
  6.5 0.1 pad_maximum_fusion.refs_0_
  6.6 0.0 collective-permute-done
  6.6 0.1 collective-permute-start.3
  6.7 2.7 %collective-permute-start.4 = (bf16[256,1792]{1,0:T(8,128)(2,1)S(1)}, bf16[256,1792]{1,0:T(8,128)(2,1)S(1)}, u32[]{:S(2)}, u32[]{:S(2)}) collective-permute-start(bf16[256,1792]{1,0:T(8,128)(2,1)S(1)} %pad_maximum_fusion.refs_0_), channel_id=1, source_target_pairs={{0,12},{1,13},{2,14},{3,15},{4,0},{5,1},{6,2},{7,3},{8,4},{9,5},{1... | collective-permute-start | bytes 2752520 | tf_op jit(solution)/shard_map/ppermute | solution.py:27
  9.4 0.9 collective-permute-start.5
  10.3 1.7 %collective-permute-start.1 = (bf16[1024,256]{1,0:T(8,128)(2,1)S(1)}, bf16[1024,256]{1,0:T(8,128)(2,1)S(1)}, u32[]{:S(2)}, u32[]{:S(2)}) collective-permute-start(bf16[1024,256]{1,0:T(8,128)(2,1)S(1)} %pad_maximum_fusion.2.refs_0_), channel_id=1, source_target_pairs={{0,32},{1,33},{2,34},{3,35},{4,36},{5,37},{6,38},{7,39},{8,40},{9,... | collective-permute-start | bytes 1572872 | tf_op jit(solution)/shard_map/ppermute | solution.py:27
  12.0 4.0 %collective-permute-start.2 = (bf16[1024,256]{1,0:T(8,128)(2,1)S(1)}, bf16[1024,256]{1,0:T(8,128)(2,1)S(1)}, u32[]{:S(2)}, u32[]{:S(2)}) collective-permute-start(bf16[1024,256]{1,0:T(8,128)(2,1)S(1)} %pad_maximum_fusion.2.refs_0_), channel_id=1, source_target_pairs={{0,224},{1,225},{2,226},{3,227},{4,228},{5,229},{6,230},{7,231},{8... | collective-permute-start | bytes 1572872 | tf_op jit(solution)/shard_map/ppermute | solution.py:27
  16.1 11.5 %collective-permute-done.1.refs_1_ = bf16[1024,256]{1,0:T(8,128)(2,1)S(1)} collective-permute-done((bf16[1024,256]{1,0:T(8,128)(2,1)S(1)}, bf16[1024,256]{1,0:T(8,128)(2,1)S(1)}, u32[]{:S(2)}, u32[]{:S(2)}) %collective-permute-start.1) | collective-permute-done | bytes 524320 | tf_op jit(solution)/shard_map/ppermute | solution.py:27
  27.6 0.0 collective-permute-done.2.refs_2_
  27.6 0.0 collective-permute-start.8
  27.6 2.7 %collective-permute-start.9 = (bf16[1024,256]{1,0:T(8,128)(2,1)S(1)}, bf16[1024,256]{1,0:T(8,128)(2,1)S(1)}, u32[]{:S(2)}, u32[]{:S(2)}) collective-permute-start(bf16[1024,256]{1,0:T(8,128)(2,1)S(1)} %collective-permute-done.2.refs_2_), channel_id=1, source_target_pairs={{0,224},{1,225},{2,226},{3,227},{4,228},{5,229},{6,230},{7,231},{8... | collective-permute-start | bytes 1572872 | tf_op jit(solution)/shard_map/ppermute | solution.py:27
  30.2 0.0 collective-permute-done.3.refs_2_
  30.2 1.7 %collective-permute-done.5.refs_1_ = bf16[256,1792]{1,0:T(8,128)(2,1)S(1)} collective-permute-done((bf16[256,1792]{1,0:T(8,128)(2,1)S(1)}, bf16[256,1792]{1,0:T(8,128)(2,1)S(1)}, u32[]{:S(2)}, u32[]{:S(2)}) %collective-permute-start.5) | collective-permute-done | bytes 917536 | tf_op jit(solution)/shard_map/ppermute | solution.py:27
  31.9 0.1 slice.36
  32.0 0.1 collective-permute-start.6
  32.1 2.7 %collective-permute-start.7 = (bf16[256,768]{1,0:T(8,128)(2,1)S(1)}, bf16[256,768]{1,0:T(8,128)(2,1)S(1)}, u32[]{:S(2)}, u32[]{:S(2)}) collective-permute-start(bf16[256,768]{1,0:T(8,128)(2,1)S(1)} %slice.37), channel_id=1, source_target_pairs={{0,12},{1,13},{2,14},{3,15},{4,0},{5,1},{6,2},{7,3},{8,4},{9,5},{1... | collective-permute-start | bytes 1179656 | tf_op jit(solution)/shard_map/ppermute | solution.py:27
  34.8 6.1 %collective-permute-done.8.refs_3_ = bf16[1024,256]{1,0:T(8,128)(2,1)S(1)} collective-permute-done((bf16[1024,256]{1,0:T(8,128)(2,1)S(1)}, bf16[1024,256]{1,0:T(8,128)(2,1)S(1)}, u32[]{:S(2)}, u32[]{:S(2)}) %collective-permute-start.8) | collective-permute-done | bytes 524320 | tf_op jit(solution)/shard_map/ppermute | solution.py:27
  40.9 0.9 collective-permute-start.10
  41.8 1.8 %collective-permute-start.11 = (bf16[1024,256]{1,0:T(8,128)(2,1)S(1)}, bf16[1024,256]{1,0:T(8,128)(2,1)S(1)}, u32[]{:S(2)}, u32[]{:S(2)}) collective-permute-start(bf16[1024,256]{1,0:T(8,128)(2,1)S(1)} %collective-permute-done.9.refs_4_), channel_id=1, source_target_pairs={{0,224},{1,225},{2,226},{3,227},{4,228},{5,229},{6,230},{7,231},{8... | collective-permute-start | bytes 1572872 | tf_op jit(solution)/shard_map/ppermute | solution.py:27
  43.6 1.6 %collective-permute-done.6.refs_4_ = bf16[256,1024]{1,0:T(8,128)(2,1)S(1)} collective-permute-done((bf16[256,1024]{1,0:T(8,128)(2,1)S(1)}, bf16[256,1024]{1,0:T(8,128)(2,1)S(1)}, u32[]{:S(2)}, u32[]{:S(2)}) %collective-permute-start.6) | collective-permute-done | bytes 524320 | tf_op jit(solution)/shard_map/ppermute | solution.py:27
  45.2 2.7 %collective-permute-start.16 = (bf16[256,1792]{1,0:T(8,128)(2,1)S(1)}, bf16[256,1792]{1,0:T(8,128)(2,1)S(1)}, u32[]{:S(2)}, u32[]{:S(2)}) collective-permute-start(bf16[256,1792]{1,0:T(8,128)(2,1)S(1)} %collective-permute-done.5.refs_1_), channel_id=1, source_target_pairs={{0,12},{1,13},{2,14},{3,15},{4,0},{5,1},{6,2},{7,3},{8,4},{9,5},{1... | collective-permute-start | bytes 2752520 | tf_op jit(solution)/shard_map/ppermute | solution.py:27
  47.9 1.2 %collective-permute-start.12 = (bf16[256,1024]{1,0:T(8,128)(2,1)S(1)}, bf16[256,1024]{1,0:T(8,128)(2,1)S(1)}, u32[]{:S(2)}, u32[]{:S(2)}) collective-permute-start(bf16[256,1024]{1,0:T(8,128)(2,1)S(1)} %collective-permute-done.6.refs_4_), channel_id=1, source_target_pairs={{0,17},{1,16},{2,19},{3,18},{4,21},{5,20},{6,23},{7,22},{8,25},{9,... | collective-permute-start | bytes 1572872 | tf_op jit(solution)/shard_map/ppermute | solution.py:27
  49.1 4.2 %collective-permute-done.10.refs_5_ = bf16[1024,256]{1,0:T(8,128)(2,1)S(1)} collective-permute-done((bf16[1024,256]{1,0:T(8,128)(2,1)S(1)}, bf16[1024,256]{1,0:T(8,128)(2,1)S(1)}, u32[]{:S(2)}, u32[]{:S(2)}) %collective-permute-start.10) | collective-permute-done | bytes 524320 | tf_op jit(solution)/shard_map/ppermute | solution.py:27
  53.4 0.5 collective-permute-start.13
  53.9 0.2 collective-permute-start.17
  54.1 6.0 %collective-permute-done.13.refs_7_ = bf16[512,256]{1,0:T(8,128)(2,1)S(1)} collective-permute-done((bf16[512,256]{1,0:T(8,128)(2,1)S(1)}, bf16[512,256]{1,0:T(8,128)(2,1)S(1)}, u32[]{:S(2)}, u32[]{:S(2)}) %collective-permute-start.13) | collective-permute-done | bytes 262176 | tf_op jit(solution)/shard_map/ppermute | solution.py:27
  60.2 1.2 %collective-permute-start.14 = (bf16[512,256]{1,0:T(8,128)(2,1)S(1)}, bf16[512,256]{1,0:T(8,128)(2,1)S(1)}, u32[]{:S(2)}, u32[]{:S(2)}) collective-permute-start(bf16[512,256]{1,0:T(8,128)(2,1)S(1)} %slice.39), channel_id=1, source_target_pairs={{0,224},{1,225},{2,226},{3,227},{4,228},{5,229},{6,230},{7,231},{8... | collective-permute-start | bytes 786440 | tf_op jit(solution)/shard_map/ppermute | solution.py:27
  61.4 4.3 %collective-permute-done.14.refs_8_ = bf16[512,256]{1,0:T(8,128)(2,1)S(1)} collective-permute-done((bf16[512,256]{1,0:T(8,128)(2,1)S(1)}, bf16[512,256]{1,0:T(8,128)(2,1)S(1)}, u32[]{:S(2)}, u32[]{:S(2)}) %collective-permute-start.14) | collective-permute-done | bytes 262176 | tf_op jit(solution)/shard_map/ppermute | solution.py:27
  65.7 0.4 shard_map.28.left
  66.1 2.0 %collective-permute-done.17.refs_7_ = bf16[256,768]{1,0:T(8,128)(2,1)S(1)} collective-permute-done((bf16[256,768]{1,0:T(8,128)(2,1)S(1)}, bf16[256,768]{1,0:T(8,128)(2,1)S(1)}, u32[]{:S(2)}, u32[]{:S(2)}) %collective-permute-start.17) | collective-permute-done | bytes 393248 | tf_op jit(solution)/shard_map/ppermute | solution.py:27
  68.0 3.4 %shard_map.29 = (f32[2,512,384]{2,1,0:T(8,128)S(1)}, bf16[2,512,384]{2,1,0:T(8,128)(2,1)S(1)}) custom-call(bf16[8,1024,256]{2,1,0:T(8,128)(2,1)S(1)} %shard_map.28.left, bf16[256,1792]{1,0:T(8,128)(2,1)S(1)} %pad_maximum_fusion.refs_0_, bf16[256,1792]{1,0:T(8,128)(2,1)S(1)} %collective-permute-done.5.refs_1_, ...), custom_call_target="tpu_custom_call" | custom-call | flops 3221225472 | bytes 10485760 | tf_op jit(solution)/shard_map/pallas_call | solution.py:111
  71.5 3.9 %collective-permute-start.20 = (bf16[2,512,384]{2,1,0:T(8,128)(2,1)S(1)}, bf16[2,512,384]{2,1,0:T(8,128)(2,1)S(1)}, u32[]{:S(2)}, u32[]{:S(2)}) collective-permute-start(bf16[2,512,384]{2,1,0:T(8,128)(2,1)S(1)} %get-tuple-element.51), channel_id=1, source_target_pairs={{0,2},{1,3},{2,0},{3,1},{4,6},{5,7},{6,4},{7,5},{8,10},{9,11},{10,... | collective-permute-start | bytes 2359304 | tf_op jit(solution)/shard_map/ppermute | solution.py:27
  75.4 4.5 %shard_map.30 = (f32[2,512,512]{2,1,0:T(8,128)S(1)}, bf16[2,512,512]{2,1,0:T(8,128)(2,1)S(1)}) custom-call(bf16[8,1024,256]{2,1,0:T(8,128)(2,1)S(1)} %shard_map.28.left, bf16[256,1792]{1,0:T(8,128)(2,1)S(1)} %pad_maximum_fusion.refs_0_, bf16[256,1792]{1,0:T(8,128)(2,1)S(1)} %collective-permute-done.5.refs_1_, ...), custom_call_target="tpu_custom_call" | custom-call | flops 4294967296 | bytes 12582912 | tf_op jit(solution)/shard_map/pallas_call | solution.py:111
  79.9 0.1 collective-permute-start.18
  80.0 0.1 fusion.3
  80.1 0.1 collective-permute-start.21
  80.2 2.5 %collective-permute-done.18 = bf16[2,512,512]{2,1,0:T(8,128)(2,1)S(1)} collective-permute-done((bf16[2,512,512]{2,1,0:T(8,128)(2,1)S(1)}, bf16[2,512,512]{2,1,0:T(8,128)(2,1)S(1)}, u32[]{:S(2)}, u32[]{:S(2)}) %collective-permute-start.18) | collective-permute-done | bytes 1048608 | tf_op jit(solution)/shard_map/ppermute | solution.py:27
  82.7 0.2 fusion.2
  82.8 0.1 collective-permute-start.19
  82.9 7.5 %collective-permute-done.21 = bf16[512,384]{1,0:T(8,128)(2,1)S(1)} collective-permute-done((bf16[512,384]{1,0:T(8,128)(2,1)S(1)}, bf16[512,384]{1,0:T(8,128)(2,1)S(1)}, u32[]{:S(2)}, u32[]{:S(2)}) %collective-permute-start.21) | collective-permute-done | bytes 393248 | tf_op jit(solution)/shard_map/ppermute | solution.py:27
  90.4 0.1 fusion.1
  90.5 11.1 %collective-permute-done.19 = bf16[512,512]{1,0:T(8,128)(2,1)S(1)} collective-permute-done((bf16[512,512]{1,0:T(8,128)(2,1)S(1)}, bf16[512,512]{1,0:T(8,128)(2,1)S(1)}, u32[]{:S(2)}, u32[]{:S(2)}) %collective-permute-start.19) | collective-permute-done | bytes 524320 | tf_op jit(solution)/shard_map/ppermute | solution.py:27
  101.6 0.2 fusion
  101.8 1.0 pad_maximum_fusion.1
  (13 shorter events, 0.1 us)
Async XLA Ops:
  1.1 5.5 %collective-permute-start = (bf16[512,256]{1,0:T(8,128)(2,1)S(1)}, bf16[512,256]{1,0:T(8,128)(2,1)S(1)}, u32[]{:S(2)}, u32[]{:S(2)}) collective-permute-start(bf16[512,256]{1,0:T(8,128)(2,1)S(1)} %get-tuple-element.62), channel_id=1, source_target_pairs={{0,2},{1,3},{2,0},{3,1},{4,6},{5,7},{6,4},{7,5},{8,10},{9,11},{10,... | collective-permute-start | bytes 786440 | tf_op jit(solution)/shard_map/ppermute | solution.py:27
  6.6 23.6 %collective-permute-start.3 = (bf16[256,1792]{1,0:T(8,128)(2,1)S(1)}, bf16[256,1792]{1,0:T(8,128)(2,1)S(1)}, u32[]{:S(2)}, u32[]{:S(2)}) collective-permute-start(bf16[256,1792]{1,0:T(8,128)(2,1)S(1)} %pad_maximum_fusion.refs_0_), channel_id=1, source_target_pairs={{0,4},{1,5},{2,6},{3,7},{4,8},{5,9},{6,10},{7,11},{8,12},{9,13},{1... | collective-permute-start | bytes 2752520 | tf_op jit(solution)/shard_map/ppermute | solution.py:27
  6.7 23.5 %collective-permute-start.4 = (bf16[256,1792]{1,0:T(8,128)(2,1)S(1)}, bf16[256,1792]{1,0:T(8,128)(2,1)S(1)}, u32[]{:S(2)}, u32[]{:S(2)}) collective-permute-start(bf16[256,1792]{1,0:T(8,128)(2,1)S(1)} %pad_maximum_fusion.refs_0_), channel_id=1, source_target_pairs={{0,12},{1,13},{2,14},{3,15},{4,0},{5,1},{6,2},{7,3},{8,4},{9,5},{1... | collective-permute-start | bytes 2752520 | tf_op jit(solution)/shard_map/ppermute | solution.py:27
  9.4 22.5 %collective-permute-start.5 = (bf16[256,1792]{1,0:T(8,128)(2,1)S(1)}, bf16[256,1792]{1,0:T(8,128)(2,1)S(1)}, u32[]{:S(2)}, u32[]{:S(2)}) collective-permute-start(bf16[256,1792]{1,0:T(8,128)(2,1)S(1)} %pad_maximum_fusion.refs_0_), channel_id=1, source_target_pairs={{0,17},{1,16},{2,19},{3,18},{4,21},{5,20},{6,23},{7,22},{8,25},{9,... | collective-permute-start | bytes 2752520 | tf_op jit(solution)/shard_map/ppermute | solution.py:27
  10.3 17.2 %collective-permute-start.1 = (bf16[1024,256]{1,0:T(8,128)(2,1)S(1)}, bf16[1024,256]{1,0:T(8,128)(2,1)S(1)}, u32[]{:S(2)}, u32[]{:S(2)}) collective-permute-start(bf16[1024,256]{1,0:T(8,128)(2,1)S(1)} %pad_maximum_fusion.2.refs_0_), channel_id=1, source_target_pairs={{0,32},{1,33},{2,34},{3,35},{4,36},{5,37},{6,38},{7,39},{8,40},{9,... | collective-permute-start | bytes 1572872 | tf_op jit(solution)/shard_map/ppermute | solution.py:27
  12.0 15.5 %collective-permute-start.2 = (bf16[1024,256]{1,0:T(8,128)(2,1)S(1)}, bf16[1024,256]{1,0:T(8,128)(2,1)S(1)}, u32[]{:S(2)}, u32[]{:S(2)}) collective-permute-start(bf16[1024,256]{1,0:T(8,128)(2,1)S(1)} %pad_maximum_fusion.2.refs_0_), channel_id=1, source_target_pairs={{0,224},{1,225},{2,226},{3,227},{4,228},{5,229},{6,230},{7,231},{8... | collective-permute-start | bytes 1572872 | tf_op jit(solution)/shard_map/ppermute | solution.py:27
  27.6 13.3 %collective-permute-start.8 = (bf16[1024,256]{1,0:T(8,128)(2,1)S(1)}, bf16[1024,256]{1,0:T(8,128)(2,1)S(1)}, u32[]{:S(2)}, u32[]{:S(2)}) collective-permute-start(bf16[1024,256]{1,0:T(8,128)(2,1)S(1)} %collective-permute-done.1.refs_1_), channel_id=1, source_target_pairs={{0,32},{1,33},{2,34},{3,35},{4,36},{5,37},{6,38},{7,39},{8,40},{9,... | collective-permute-start | bytes 1572872 | tf_op jit(solution)/shard_map/ppermute | solution.py:27
  27.6 13.3 %collective-permute-start.9 = (bf16[1024,256]{1,0:T(8,128)(2,1)S(1)}, bf16[1024,256]{1,0:T(8,128)(2,1)S(1)}, u32[]{:S(2)}, u32[]{:S(2)}) collective-permute-start(bf16[1024,256]{1,0:T(8,128)(2,1)S(1)} %collective-permute-done.2.refs_2_), channel_id=1, source_target_pairs={{0,224},{1,225},{2,226},{3,227},{4,228},{5,229},{6,230},{7,231},{8... | collective-permute-start | bytes 1572872 | tf_op jit(solution)/shard_map/ppermute | solution.py:27
  32.0 13.3 %collective-permute-start.6 = (bf16[256,1024]{1,0:T(8,128)(2,1)S(1)}, bf16[256,1024]{1,0:T(8,128)(2,1)S(1)}, u32[]{:S(2)}, u32[]{:S(2)}) collective-permute-start(bf16[256,1024]{1,0:T(8,128)(2,1)S(1)} %slice.36), channel_id=1, source_target_pairs={{0,4},{1,5},{2,6},{3,7},{4,8},{5,9},{6,10},{7,11},{8,12},{9,13},{1... | collective-permute-start | bytes 1572872 | tf_op jit(solution)/shard_map/ppermute | solution.py:27
  32.1 11.5 %collective-permute-start.7 = (bf16[256,768]{1,0:T(8,128)(2,1)S(1)}, bf16[256,768]{1,0:T(8,128)(2,1)S(1)}, u32[]{:S(2)}, u32[]{:S(2)}) collective-permute-start(bf16[256,768]{1,0:T(8,128)(2,1)S(1)} %slice.37), channel_id=1, source_target_pairs={{0,12},{1,13},{2,14},{3,15},{4,0},{5,1},{6,2},{7,3},{8,4},{9,5},{1... | collective-permute-start | bytes 1179656 | tf_op jit(solution)/shard_map/ppermute | solution.py:27
  40.9 12.4 %collective-permute-start.10 = (bf16[1024,256]{1,0:T(8,128)(2,1)S(1)}, bf16[1024,256]{1,0:T(8,128)(2,1)S(1)}, u32[]{:S(2)}, u32[]{:S(2)}) collective-permute-start(bf16[1024,256]{1,0:T(8,128)(2,1)S(1)} %collective-permute-done.8.refs_3_), channel_id=1, source_target_pairs={{0,32},{1,33},{2,34},{3,35},{4,36},{5,37},{6,38},{7,39},{8,40},{9,... | collective-permute-start | bytes 1572872 | tf_op jit(solution)/shard_map/ppermute | solution.py:27
  41.8 11.5 %collective-permute-start.11 = (bf16[1024,256]{1,0:T(8,128)(2,1)S(1)}, bf16[1024,256]{1,0:T(8,128)(2,1)S(1)}, u32[]{:S(2)}, u32[]{:S(2)}) collective-permute-start(bf16[1024,256]{1,0:T(8,128)(2,1)S(1)} %collective-permute-done.9.refs_4_), channel_id=1, source_target_pairs={{0,224},{1,225},{2,226},{3,227},{4,228},{5,229},{6,230},{7,231},{8... | collective-permute-start | bytes 1572872 | tf_op jit(solution)/shard_map/ppermute | solution.py:27
  45.2 22.8 %collective-permute-start.15 = (bf16[256,1792]{1,0:T(8,128)(2,1)S(1)}, bf16[256,1792]{1,0:T(8,128)(2,1)S(1)}, u32[]{:S(2)}, u32[]{:S(2)}) collective-permute-start(bf16[256,1792]{1,0:T(8,128)(2,1)S(1)} %collective-permute-done.5.refs_1_), channel_id=1, source_target_pairs={{0,4},{1,5},{2,6},{3,7},{4,8},{5,9},{6,10},{7,11},{8,12},{9,13},{1... | collective-permute-start | bytes 2752520 | tf_op jit(solution)/shard_map/ppermute | solution.py:27
  45.2 22.8 %collective-permute-start.16 = (bf16[256,1792]{1,0:T(8,128)(2,1)S(1)}, bf16[256,1792]{1,0:T(8,128)(2,1)S(1)}, u32[]{:S(2)}, u32[]{:S(2)}) collective-permute-start(bf16[256,1792]{1,0:T(8,128)(2,1)S(1)} %collective-permute-done.5.refs_1_), channel_id=1, source_target_pairs={{0,12},{1,13},{2,14},{3,15},{4,0},{5,1},{6,2},{7,3},{8,4},{9,5},{1... | collective-permute-start | bytes 2752520 | tf_op jit(solution)/shard_map/ppermute | solution.py:27
  47.9 13.4 %collective-permute-start.12 = (bf16[256,1024]{1,0:T(8,128)(2,1)S(1)}, bf16[256,1024]{1,0:T(8,128)(2,1)S(1)}, u32[]{:S(2)}, u32[]{:S(2)}) collective-permute-start(bf16[256,1024]{1,0:T(8,128)(2,1)S(1)} %collective-permute-done.6.refs_4_), channel_id=1, source_target_pairs={{0,17},{1,16},{2,19},{3,18},{4,21},{5,20},{6,23},{7,22},{8,25},{9,... | collective-permute-start | bytes 1572872 | tf_op jit(solution)/shard_map/ppermute | solution.py:27
  53.4 6.8 %collective-permute-start.13 = (bf16[512,256]{1,0:T(8,128)(2,1)S(1)}, bf16[512,256]{1,0:T(8,128)(2,1)S(1)}, u32[]{:S(2)}, u32[]{:S(2)}) collective-permute-start(bf16[512,256]{1,0:T(8,128)(2,1)S(1)} %slice.38), channel_id=1, source_target_pairs={{0,32},{1,33},{2,34},{3,35},{4,36},{5,37},{6,38},{7,39},{8,40},{9,... | collective-permute-start | bytes 786440 | tf_op jit(solution)/shard_map/ppermute | solution.py:27
  53.9 14.1 %collective-permute-start.17 = (bf16[256,768]{1,0:T(8,128)(2,1)S(1)}, bf16[256,768]{1,0:T(8,128)(2,1)S(1)}, u32[]{:S(2)}, u32[]{:S(2)}) collective-permute-start(bf16[256,768]{1,0:T(8,128)(2,1)S(1)} %collective-permute-done.7.refs_4_), channel_id=1, source_target_pairs={{0,17},{1,16},{2,19},{3,18},{4,21},{5,20},{6,23},{7,22},{8,25},{9,... | collective-permute-start | bytes 1179656 | tf_op jit(solution)/shard_map/ppermute | solution.py:27
  60.2 5.5 %collective-permute-start.14 = (bf16[512,256]{1,0:T(8,128)(2,1)S(1)}, bf16[512,256]{1,0:T(8,128)(2,1)S(1)}, u32[]{:S(2)}, u32[]{:S(2)}) collective-permute-start(bf16[512,256]{1,0:T(8,128)(2,1)S(1)} %slice.39), channel_id=1, source_target_pairs={{0,224},{1,225},{2,226},{3,227},{4,228},{5,229},{6,230},{7,231},{8... | collective-permute-start | bytes 786440 | tf_op jit(solution)/shard_map/ppermute | solution.py:27
  71.5 8.5 %collective-permute-start.20 = (bf16[2,512,384]{2,1,0:T(8,128)(2,1)S(1)}, bf16[2,512,384]{2,1,0:T(8,128)(2,1)S(1)}, u32[]{:S(2)}, u32[]{:S(2)}) collective-permute-start(bf16[2,512,384]{2,1,0:T(8,128)(2,1)S(1)} %get-tuple-element.51), channel_id=1, source_target_pairs={{0,2},{1,3},{2,0},{3,1},{4,6},{5,7},{6,4},{7,5},{8,10},{9,11},{10,... | collective-permute-start | bytes 2359304 | tf_op jit(solution)/shard_map/ppermute | solution.py:27
  79.9 2.7 %collective-permute-start.18 = (bf16[2,512,512]{2,1,0:T(8,128)(2,1)S(1)}, bf16[2,512,512]{2,1,0:T(8,128)(2,1)S(1)}, u32[]{:S(2)}, u32[]{:S(2)}) collective-permute-start(bf16[2,512,512]{2,1,0:T(8,128)(2,1)S(1)} %get-tuple-element.55), channel_id=1, source_target_pairs={{0,2},{1,3},{2,0},{3,1},{4,6},{5,7},{6,4},{7,5},{8,10},{9,11},{10,... | collective-permute-start | bytes 3145736 | tf_op jit(solution)/shard_map/ppermute | solution.py:27
  80.1 10.3 %collective-permute-start.21 = (bf16[512,384]{1,0:T(8,128)(2,1)S(1)}, bf16[512,384]{1,0:T(8,128)(2,1)S(1)}, u32[]{:S(2)}, u32[]{:S(2)}) collective-permute-start(bf16[512,384]{1,0:T(8,128)(2,1)S(1)} %fusion.3), channel_id=1, source_target_pairs={{0,1},{1,0},{2,3},{3,2},{4,5},{5,4},{6,7},{7,6},{8,9},{9,8},{10,11... | collective-permute-start | bytes 1179656 | tf_op jit(solution)/shard_map/ppermute | solution.py:27
  82.8 18.8 %collective-permute-start.19 = (bf16[512,512]{1,0:T(8,128)(2,1)S(1)}, bf16[512,512]{1,0:T(8,128)(2,1)S(1)}, u32[]{:S(2)}, u32[]{:S(2)}) collective-permute-start(bf16[512,512]{1,0:T(8,128)(2,1)S(1)} %fusion.2), channel_id=1, source_target_pairs={{0,1},{1,0},{2,3},{3,2},{4,5},{5,4},{6,7},{7,6},{8,9},{9,8},{10,11... | collective-permute-start | bytes 1572872 | tf_op jit(solution)/shard_map/ppermute | solution.py:27

commit v3 on v2

--- a/solution.py
+++ b/solution.py
@@ -83,43 +83,38 @@
     )(*values)
 
 
-def product_kernel(places, left, *refs):
+def product_kernel(places, block, left, *refs):
     rights = refs[:len(places)]
-    keep, send, total = refs[len(places):]
-    _, rows, share = keep.shape
+    target, total = refs[len(places):]
+    _, rows, share = target.shape
     col = lax.axis_index("col")
     x_lo = lax.axis_index("depth")
     x_hi, y = col // (2 * Y), col // 2 % Y
-    for block in (1, 0):
-        for index, (side, dy, first) in enumerate(places):
-            place = lax.rem(x_hi + side, X) * Y + lax.rem(y + dy, Y)
-            term = jnp.dot(
-                left[place, block * rows:(block + 1) * rows],
-                rights[index][:, first:first + 2 * share],
-                preferred_element_type=jnp.float32,
-            )
-            total[...] = total[...] + term if index else term
-        for d in range(2):
-            target = send if block else keep
-            target[lax.rem(x_lo + d, 2)] = total[:, d * share:(d + 1) * share].astype(target.dtype)
-
-
-def product(left, pieces, columns):
+    for index, (side, dy, first) in enumerate(places):
+        place = lax.rem(x_hi + side, X) * Y + lax.rem(y + dy, Y)
+        term = jnp.dot(
+            left[place, block * rows:(block + 1) * rows],
+            rights[index][:, first:first + 2 * share],
+            preferred_element_type=jnp.float32,
+        )
+        total[...] = total[...] + term if index else term
+    for d in range(2):
+        target[lax.rem(x_lo + d, 2)] = total[:, d * share:(d + 1) * share].astype(target.dtype)
+
+
+def product(left, pieces, columns, block):
     values, places = zip(*pieces)
     rows, inner = left.shape[1] // 2, left.shape[0] * left.shape[2]
     vmem = pl.BlockSpec(memory_space=pltpu.VMEM)
     return pl.pallas_call(
-        functools.partial(product_kernel, places),
-        out_shape=(
-            jax.ShapeDtypeStruct((2, rows, columns // 2), jnp.float32),
-            jax.ShapeDtypeStruct((2, rows, columns // 2), jnp.bfloat16),
-        ),
+        functools.partial(product_kernel, places, block),
+        out_shape=jax.ShapeDtypeStruct((2, rows, columns // 2), jnp.bfloat16 if block else jnp.float32),
         in_specs=[vmem] * (1 + len(values)),
-        out_specs=(vmem, vmem),
+        out_specs=vmem,
         scratch_shapes=[pltpu.VMEM((rows, columns), jnp.float32)],
         compiler_params=pltpu.CompilerParams(vmem_limit_bytes=24 * 1024 * 1024),
         cost_estimate=pl.CostEstimate(
-            flops=4 * rows * inner * columns, bytes_accessed=4 * inner * (rows + columns), transcendentals=0
+            flops=2 * rows * inner * columns, bytes_accessed=2 * inner * (rows + columns), transcendentals=0
         ),
     )(left, *values)
 
@@ -197,17 +192,22 @@
                 ("u3", 0, Z - 3), ("d3", 0, 3), ("u4", 0, Z // 2), ("d4", 1, Z // 2)]
     gate("nfa", "u4")
     left = packed_left([(values[k], tuple(v)) for k, *v in a_pieces], rows)
+    pieces, sizes, came = {}, {}, {}
+    for chunk, first in (("b", 2 * wide), ("a", 0)):
+        names = [("o", 0, 0, first), ("n", 1, 0, first), ("u", 0, Y - 1, first), ("d", 0, 1, first), ("f" + chunk, 0, 2, 0),
+                 ("nu", 1, Y - 1, first), ("nd", 1, 1, first), ("nf" + chunk, 1, 2, 0)]
+        pieces[chunk] = [(values[k], tuple(v)) for k, *v in names]
+        sizes[chunk] = values["f" + chunk].shape[1]
+        send = product(left, pieces[chunk], sizes[chunk], 1)
+        came[chunk] = moved(send, sibling)
+        left, _ = lax.optimization_barrier((left, send))
     parts = []
-    for chunk, first in (("b", 2 * wide), ("a", 0)):
-        b_pieces = [("o", 0, 0, first), ("n", 1, 0, first), ("u", 0, Y - 1, first), ("d", 0, 1, first), ("f" + chunk, 0, 2, 0),
-                    ("nu", 1, Y - 1, first), ("nd", 1, 1, first), ("nf" + chunk, 1, 2, 0)]
-        keep, send = product(left, [(values[k], tuple(v)) for k, *v in b_pieces],
-                             values["f" + chunk].shape[1])
-        came = moved(send, sibling)
-        left, _ = lax.optimization_barrier((left, send))
-        away = (keep[1] + came[1].astype(jnp.float32)).astype(jnp.bfloat16)
+    for chunk in "ba":
+        keep = product(left, pieces[chunk], sizes[chunk], 0)
+        away = (keep[1] + came[chunk][1].astype(jnp.float32)).astype(jnp.bfloat16)
         arrived = moved(away, x_pair)
-        parts.append((keep[0] + came[0].astype(jnp.float32) + arrived.astype(jnp.float32)).astype(jnp.bfloat16))
+        left, _ = lax.optimization_barrier((left, away))
+        parts.append((keep[0] + came[chunk][0].astype(jnp.float32) + arrived.astype(jnp.float32)).astype(jnp.bfloat16))
     first = lax.pad(parts[0], jnp.zeros((), jnp.bfloat16), ((0, 0, 0), (wide, 0, 0)))
     return lax.dynamic_update_slice(first, parts[1], (0, 0))
 

time: 103 us -> 101 us (0.981)
  waiting for transfers between devices: 58.4 us -> 54.7 us
  starting transfers between devices: 30.9 us -> 32.4 us
    ppermute x22, waiting for transfers between devices: 58.4 us -> 54.7 us  [moved(): return lax.ppermute(value, AXES, pairs)]
    ppermute x22, starting transfers between devices: 30.9 us -> 32.4 us  [moved(): return lax.ppermute(value, AXES, pairs)]
    pallas_call x2 -> x4, Pallas kernels: 7.92 us -> 8.24 us  [product(): pl.pallas_call(functools.partial(product_kernel, places, block), out_shap...]
  transfers between devices with their start and end apart: 22 -> 22, of which waited for: 11 -> 10; matrix products, arithmetic and copies ran while one was open for 3% -> 3% of each run, Pallas kernels for 5% -> 7%
where the time goes in v3:
time: 101 us
  waiting for transfers between devices  54.7 us (54%)
  starting transfers between devices  32.4 us (32%)
  Pallas kernels  8.63 us (9%)
  local copies, waits for them, and re-layouts  3.32 us (3%)
  other arithmetic  1.67 us (2%)
    ppermute x22, waiting for transfers between devices, moved(): return lax.ppermute(value, AXES, pairs)  54.7 us
    ppermute x22, starting transfers between devices, moved(): return lax.ppermute(value, AXES, pairs)  32.4 us
    pallas_call x4, Pallas kernels, product(): pl.pallas_call(functools.partial(product_kernel, places, block), out_shap...  8.24 us
    dynamic_slice x2, local copies, waits for them, and re-layouts, cut(): lax.dynamic_slice(b_matrix, (part * half, d * share + first), (half, width))  2.14 us
  transfers between devices with their start and end apart: 22, of which 10 were waited for; matrix products, arithmetic and copies ran while one was open for 3% of the time, Pallas kernels for 7%

profile of v3, /device:TPU:1, one launch (start us, length us, event | category | flops | bytes accessed | tf_op | source)
XLA Modules:
  0.0 100.8 jit_solution(7122594370675607272)
XLA Ops:
  0.0 1.1 %constant_dynamic-slice_fusion.2 = (bf16[512,256]{1,0:T(8,128)(2,1)S(1)}, bf16[512,256]{1,0:T(8,128)(2,1)S(1)}) fusion(bf16[512,1024]{1,0:T(8,128)(2,1)} %param.2, s32[]{:T(128)S(6)} %select_n.25, s32[]{:T(128)S(6)} %select_n.26), kind=kLoop, calls=%fused_computation.19 | loop fusion | bytes 1048584 | tf_op jit(solution)/shard_map/dynamic_slice | solution.py:154
  1.1 3.3 %collective-permute-start = (bf16[512,256]{1,0:T(8,128)(2,1)S(1)}, bf16[512,256]{1,0:T(8,128)(2,1)S(1)}, u32[]{:S(2)}, u32[]{:S(2)}) collective-permute-start(bf16[512,256]{1,0:T(8,128)(2,1)S(1)} %get-tuple-element.58), channel_id=1, source_target_pairs={{0,2},{1,3},{2,0},{3,1},{4,6},{5,7},{6,4},{7,5},{8,10},{9,11},{10,... | collective-permute-start | bytes 786440 | tf_op jit(solution)/shard_map/ppermute | solution.py:27
  4.4 1.1 %constant_dynamic-slice_fusion = (bf16[256,512]{1,0:T(8,128)(2,1)S(1)}, bf16[256,512]{1,0:T(8,128)(2,1)S(1)}) fusion(bf16[512,1792]{1,0:T(8,128)(2,1)} %param.3, s32[]{:T(128)S(6)} %select_n.27), kind=kLoop, calls=%fused_computation.17 | loop fusion | bytes 1048580 | tf_op jit(solution)/shard_map/dynamic_slice | solution.py:150
  5.5 1.1 %constant_dynamic-slice_fusion.5 = (bf16[256,384]{1,0:T(8,128)(2,1)S(1)}, bf16[256,384]{1,0:T(8,128)(2,1)S(1)}) fusion(bf16[512,1792]{1,0:T(8,128)(2,1)} %param.3, s32[]{:T(128)S(6)} %select_n.27), kind=kLoop, calls=%fused_computation.22 | loop fusion | bytes 786436 | tf_op jit(solution)/shard_map/dynamic_slice | solution.py:150
  6.5 0.1 pad_maximum_fusion.refs_0_
  6.6 0.1 collective-permute-start.3
  6.7 2.7 %collective-permute-start.4 = (bf16[256,1792]{1,0:T(8,128)(2,1)S(1)}, bf16[256,1792]{1,0:T(8,128)(2,1)S(1)}, u32[]{:S(2)}, u32[]{:S(2)}) collective-permute-start(bf16[256,1792]{1,0:T(8,128)(2,1)S(1)} %pad_maximum_fusion.refs_0_), channel_id=1, source_target_pairs={{0,12},{1,13},{2,14},{3,15},{4,0},{5,1},{6,2},{7,3},{8,4},{9,5},{1... | collective-permute-start | bytes 2752520 | tf_op jit(solution)/shard_map/ppermute | solution.py:27
  9.4 0.9 collective-permute-start.5
  10.3 1.7 %collective-permute-start.1 = (bf16[1024,256]{1,0:T(8,128)(2,1)S(1)}, bf16[1024,256]{1,0:T(8,128)(2,1)S(1)}, u32[]{:S(2)}, u32[]{:S(2)}) collective-permute-start(bf16[1024,256]{1,0:T(8,128)(2,1)S(1)} %pad_maximum_fusion.2.refs_0_), channel_id=1, source_target_pairs={{0,32},{1,33},{2,34},{3,35},{4,36},{5,37},{6,38},{7,39},{8,40},{9,... | collective-permute-start | bytes 1572872 | tf_op jit(solution)/shard_map/ppermute | solution.py:27
  12.0 4.0 %collective-permute-start.2 = (bf16[1024,256]{1,0:T(8,128)(2,1)S(1)}, bf16[1024,256]{1,0:T(8,128)(2,1)S(1)}, u32[]{:S(2)}, u32[]{:S(2)}) collective-permute-start(bf16[1024,256]{1,0:T(8,128)(2,1)S(1)} %pad_maximum_fusion.2.refs_0_), channel_id=1, source_target_pairs={{0,224},{1,225},{2,226},{3,227},{4,228},{5,229},{6,230},{7,231},{8... | collective-permute-start | bytes 1572872 | tf_op jit(solution)/shard_map/ppermute | solution.py:27
  16.1 11.5 %collective-permute-done.1.refs_1_ = bf16[1024,256]{1,0:T(8,128)(2,1)S(1)} collective-permute-done((bf16[1024,256]{1,0:T(8,128)(2,1)S(1)}, bf16[1024,256]{1,0:T(8,128)(2,1)S(1)}, u32[]{:S(2)}, u32[]{:S(2)}) %collective-permute-start.1) | collective-permute-done | bytes 524320 | tf_op jit(solution)/shard_map/ppermute | solution.py:27
  27.6 0.0 collective-permute-done.2.refs_2_
  27.6 0.0 collective-permute-start.8
  27.6 2.7 %collective-permute-start.9 = (bf16[1024,256]{1,0:T(8,128)(2,1)S(1)}, bf16[1024,256]{1,0:T(8,128)(2,1)S(1)}, u32[]{:S(2)}, u32[]{:S(2)}) collective-permute-start(bf16[1024,256]{1,0:T(8,128)(2,1)S(1)} %collective-permute-done.2.refs_2_), channel_id=1, source_target_pairs={{0,224},{1,225},{2,226},{3,227},{4,228},{5,229},{6,230},{7,231},{8... | collective-permute-start | bytes 1572872 | tf_op jit(solution)/shard_map/ppermute | solution.py:27
  30.2 0.0 collective-permute-done.3.refs_2_
  30.2 1.7 %collective-permute-done.5.refs_1_ = bf16[256,1792]{1,0:T(8,128)(2,1)S(1)} collective-permute-done((bf16[256,1792]{1,0:T(8,128)(2,1)S(1)}, bf16[256,1792]{1,0:T(8,128)(2,1)S(1)}, u32[]{:S(2)}, u32[]{:S(2)}) %collective-permute-start.5) | collective-permute-done | bytes 917536 | tf_op jit(solution)/shard_map/ppermute | solution.py:27
  31.9 0.1 slice.36
  32.0 0.1 collective-permute-start.6
  32.1 2.7 %collective-permute-start.7 = (bf16[256,768]{1,0:T(8,128)(2,1)S(1)}, bf16[256,768]{1,0:T(8,128)(2,1)S(1)}, u32[]{:S(2)}, u32[]{:S(2)}) collective-permute-start(bf16[256,768]{1,0:T(8,128)(2,1)S(1)} %slice.37), channel_id=1, source_target_pairs={{0,12},{1,13},{2,14},{3,15},{4,0},{5,1},{6,2},{7,3},{8,4},{9,5},{1... | collective-permute-start | bytes 1179656 | tf_op jit(solution)/shard_map/ppermute | solution.py:27
  34.8 6.1 %collective-permute-done.8.refs_3_ = bf16[1024,256]{1,0:T(8,128)(2,1)S(1)} collective-permute-done((bf16[1024,256]{1,0:T(8,128)(2,1)S(1)}, bf16[1024,256]{1,0:T(8,128)(2,1)S(1)}, u32[]{:S(2)}, u32[]{:S(2)}) %collective-permute-start.8) | collective-permute-done | bytes 524320 | tf_op jit(solution)/shard_map/ppermute | solution.py:27
  40.9 0.9 collective-permute-start.10
  41.8 1.8 %collective-permute-start.11 = (bf16[1024,256]{1,0:T(8,128)(2,1)S(1)}, bf16[1024,256]{1,0:T(8,128)(2,1)S(1)}, u32[]{:S(2)}, u32[]{:S(2)}) collective-permute-start(bf16[1024,256]{1,0:T(8,128)(2,1)S(1)} %collective-permute-done.9.refs_4_), channel_id=1, source_target_pairs={{0,224},{1,225},{2,226},{3,227},{4,228},{5,229},{6,230},{7,231},{8... | collective-permute-start | bytes 1572872 | tf_op jit(solution)/shard_map/ppermute | solution.py:27
  43.6 1.6 %collective-permute-done.6.refs_4_ = bf16[256,1024]{1,0:T(8,128)(2,1)S(1)} collective-permute-done((bf16[256,1024]{1,0:T(8,128)(2,1)S(1)}, bf16[256,1024]{1,0:T(8,128)(2,1)S(1)}, u32[]{:S(2)}, u32[]{:S(2)}) %collective-permute-start.6) | collective-permute-done | bytes 524320 | tf_op jit(solution)/shard_map/ppermute | solution.py:27
  45.2 2.7 %collective-permute-start.16 = (bf16[256,1792]{1,0:T(8,128)(2,1)S(1)}, bf16[256,1792]{1,0:T(8,128)(2,1)S(1)}, u32[]{:S(2)}, u32[]{:S(2)}) collective-permute-start(bf16[256,1792]{1,0:T(8,128)(2,1)S(1)} %collective-permute-done.5.refs_1_), channel_id=1, source_target_pairs={{0,12},{1,13},{2,14},{3,15},{4,0},{5,1},{6,2},{7,3},{8,4},{9,5},{1... | collective-permute-start | bytes 2752520 | tf_op jit(solution)/shard_map/ppermute | solution.py:27
  47.9 1.2 %collective-permute-start.12 = (bf16[256,1024]{1,0:T(8,128)(2,1)S(1)}, bf16[256,1024]{1,0:T(8,128)(2,1)S(1)}, u32[]{:S(2)}, u32[]{:S(2)}) collective-permute-start(bf16[256,1024]{1,0:T(8,128)(2,1)S(1)} %collective-permute-done.6.refs_4_), channel_id=1, source_target_pairs={{0,17},{1,16},{2,19},{3,18},{4,21},{5,20},{6,23},{7,22},{8,25},{9,... | collective-permute-start | bytes 1572872 | tf_op jit(solution)/shard_map/ppermute | solution.py:27
  49.1 4.2 %collective-permute-done.10.refs_5_ = bf16[1024,256]{1,0:T(8,128)(2,1)S(1)} collective-permute-done((bf16[1024,256]{1,0:T(8,128)(2,1)S(1)}, bf16[1024,256]{1,0:T(8,128)(2,1)S(1)}, u32[]{:S(2)}, u32[]{:S(2)}) %collective-permute-start.10) | collective-permute-done | bytes 524320 | tf_op jit(solution)/shard_map/ppermute | solution.py:27
  53.4 0.5 collective-permute-start.13
  53.9 0.2 collective-permute-start.17
  54.1 6.0 %collective-permute-done.13.refs_7_ = bf16[512,256]{1,0:T(8,128)(2,1)S(1)} collective-permute-done((bf16[512,256]{1,0:T(8,128)(2,1)S(1)}, bf16[512,256]{1,0:T(8,128)(2,1)S(1)}, u32[]{:S(2)}, u32[]{:S(2)}) %collective-permute-start.13) | collective-permute-done | bytes 262176 | tf_op jit(solution)/shard_map/ppermute | solution.py:27
  60.2 1.2 %collective-permute-start.14 = (bf16[512,256]{1,0:T(8,128)(2,1)S(1)}, bf16[512,256]{1,0:T(8,128)(2,1)S(1)}, u32[]{:S(2)}, u32[]{:S(2)}) collective-permute-start(bf16[512,256]{1,0:T(8,128)(2,1)S(1)} %slice.39), channel_id=1, source_target_pairs={{0,224},{1,225},{2,226},{3,227},{4,228},{5,229},{6,230},{7,231},{8... | collective-permute-start | bytes 786440 | tf_op jit(solution)/shard_map/ppermute | solution.py:27
  61.4 4.3 %collective-permute-done.14.refs_8_ = bf16[512,256]{1,0:T(8,128)(2,1)S(1)} collective-permute-done((bf16[512,256]{1,0:T(8,128)(2,1)S(1)}, bf16[512,256]{1,0:T(8,128)(2,1)S(1)}, u32[]{:S(2)}, u32[]{:S(2)}) %collective-permute-start.14) | collective-permute-done | bytes 262176 | tf_op jit(solution)/shard_map/ppermute | solution.py:27
  65.7 0.4 shard_map.28.left
  66.1 2.0 %collective-permute-done.17.refs_7_ = bf16[256,768]{1,0:T(8,128)(2,1)S(1)} collective-permute-done((bf16[256,768]{1,0:T(8,128)(2,1)S(1)}, bf16[256,768]{1,0:T(8,128)(2,1)S(1)}, u32[]{:S(2)}, u32[]{:S(2)}) %collective-permute-start.17) | collective-permute-done | bytes 393248 | tf_op jit(solution)/shard_map/ppermute | solution.py:27
  68.0 1.8 %shard_map.29 = bf16[2,512,384]{2,1,0:T(8,128)(2,1)S(1)} custom-call(bf16[8,1024,256]{2,1,0:T(8,128)(2,1)S(1)} %shard_map.28.left, bf16[256,1792]{1,0:T(8,128)(2,1)S(1)} %pad_maximum_fusion.refs_0_, bf16[256,1792]{1,0:T(8,128)(2,1)S(1)} %collective-permute-done.5.refs_1_, bf16[256,1792]{1,0:T(8,128)(2,1)S(1)} %collective-permute-done.3.refs_2_, ...), custom_call_target="tpu_custom_call" | custom-call | flops 1610612736 | bytes 5242880 | tf_op jit(solution)/shard_map/pallas_call | solution.py:109
  69.8 3.9 %collective-permute-start.18 = (bf16[2,512,384]{2,1,0:T(8,128)(2,1)S(1)}, bf16[2,512,384]{2,1,0:T(8,128)(2,1)S(1)}, u32[]{:S(2)}, u32[]{:S(2)}) collective-permute-start(bf16[2,512,384]{2,1,0:T(8,128)(2,1)S(1)} %shard_map.29), channel_id=1, source_target_pairs={{0,2},{1,3},{2,0},{3,1},{4,6},{5,7},{6,4},{7,5},{8,10},{9,11},{10,... | collective-permute-start | bytes 2359304 | tf_op jit(solution)/shard_map/ppermute | solution.py:27
  73.8 2.3 %shard_map.30 = bf16[2,512,512]{2,1,0:T(8,128)(2,1)S(1)} custom-call(bf16[8,1024,256]{2,1,0:T(8,128)(2,1)S(1)} %shard_map.28.left, bf16[256,1792]{1,0:T(8,128)(2,1)S(1)} %pad_maximum_fusion.refs_0_, bf16[256,1792]{1,0:T(8,128)(2,1)S(1)} %collective-permute-done.5.refs_1_, bf16[256,1792]{1,0:T(8,128)(2,1)S(1)} %collective-permute-done.3.refs_2_, ...), custom_call_target="tpu_custom_call" | custom-call | flops 2147483648 | bytes 6291456 | tf_op jit(solution)/shard_map/pallas_call | solution.py:109
  76.1 0.1 collective-permute-start.19
  76.2 1.8 %shard_map.31 = f32[2,512,384]{2,1,0:T(8,128)S(1)} custom-call(bf16[8,1024,256]{2,1,0:T(8,128)(2,1)S(1)} %shard_map.28.left, bf16[256,1792]{1,0:T(8,128)(2,1)S(1)} %pad_maximum_fusion.refs_0_, bf16[256,1792]{1,0:T(8,128)(2,1)S(1)} %collective-permute-done.5.refs_1_, bf16[256,1792]{1,0:T(8,128)(2,1)S(1)} %collective-permute-done.3.refs_2_, ...), custom_call_target="tpu_custom_call" | custom-call | flops 1610612736 | bytes 5242880 | tf_op jit(solution)/shard_map/pallas_call | solution.py:109
  78.0 0.1 fusion.9
  78.1 0.1 collective-permute-start.21
  78.2 2.3 %shard_map.32 = f32[2,512,512]{2,1,0:T(8,128)S(1)} custom-call(bf16[8,1024,256]{2,1,0:T(8,128)(2,1)S(1)} %shard_map.28.left, bf16[256,1792]{1,0:T(8,128)(2,1)S(1)} %pad_maximum_fusion.refs_0_, bf16[256,1792]{1,0:T(8,128)(2,1)S(1)} %collective-permute-done.5.refs_1_, bf16[256,1792]{1,0:T(8,128)(2,1)S(1)} %collective-permute-done.3.refs_2_, ...), custom_call_target="tpu_custom_call" | custom-call | flops 2147483648 | bytes 6291456 | tf_op jit(solution)/shard_map/pallas_call | solution.py:109
  80.6 0.2 fusion.8
  80.7 1.5 %collective-permute-start.20 = (bf16[512,512]{1,0:T(8,128)(2,1)S(1)}, bf16[512,512]{1,0:T(8,128)(2,1)S(1)}, u32[]{:S(2)}, u32[]{:S(2)}) collective-permute-start(bf16[512,512]{1,0:T(8,128)(2,1)S(1)} %fusion.8), channel_id=1, source_target_pairs={{0,1},{1,0},{2,3},{3,2},{4,5},{5,4},{6,7},{7,6},{8,9},{9,8},{10,11... | collective-permute-start | bytes 1572872 | tf_op jit(solution)/shard_map/ppermute | solution.py:27
  82.3 6.1 %collective-permute-done.21 = bf16[512,384]{1,0:T(8,128)(2,1)S(1)} collective-permute-done((bf16[512,384]{1,0:T(8,128)(2,1)S(1)}, bf16[512,384]{1,0:T(8,128)(2,1)S(1)}, u32[]{:S(2)}, u32[]{:S(2)}) %collective-permute-start.21) | collective-permute-done | bytes 393248 | tf_op jit(solution)/shard_map/ppermute | solution.py:27
  88.4 0.1 fusion.6
  88.5 11.1 %collective-permute-done.20 = bf16[512,512]{1,0:T(8,128)(2,1)S(1)} collective-permute-done((bf16[512,512]{1,0:T(8,128)(2,1)S(1)}, bf16[512,512]{1,0:T(8,128)(2,1)S(1)}, u32[]{:S(2)}, u32[]{:S(2)}) %collective-permute-start.20) | collective-permute-done | bytes 524320 | tf_op jit(solution)/shard_map/ppermute | solution.py:27
  99.6 0.2 fusion.3
  99.8 1.0 pad_maximum_fusion.1
  (15 shorter events, 0.1 us)
Async XLA Ops:
  1.1 5.5 %collective-permute-start = (bf16[512,256]{1,0:T(8,128)(2,1)S(1)}, bf16[512,256]{1,0:T(8,128)(2,1)S(1)}, u32[]{:S(2)}, u32[]{:S(2)}) collective-permute-start(bf16[512,256]{1,0:T(8,128)(2,1)S(1)} %get-tuple-element.58), channel_id=1, source_target_pairs={{0,2},{1,3},{2,0},{3,1},{4,6},{5,7},{6,4},{7,5},{8,10},{9,11},{10,... | collective-permute-start | bytes 786440 | tf_op jit(solution)/shard_map/ppermute | solution.py:27
  6.6 23.6 %collective-permute-start.3 = (bf16[256,1792]{1,0:T(8,128)(2,1)S(1)}, bf16[256,1792]{1,0:T(8,128)(2,1)S(1)}, u32[]{:S(2)}, u32[]{:S(2)}) collective-permute-start(bf16[256,1792]{1,0:T(8,128)(2,1)S(1)} %pad_maximum_fusion.refs_0_), channel_id=1, source_target_pairs={{0,4},{1,5},{2,6},{3,7},{4,8},{5,9},{6,10},{7,11},{8,12},{9,13},{1... | collective-permute-start | bytes 2752520 | tf_op jit(solution)/shard_map/ppermute | solution.py:27
  6.7 23.5 %collective-permute-start.4 = (bf16[256,1792]{1,0:T(8,128)(2,1)S(1)}, bf16[256,1792]{1,0:T(8,128)(2,1)S(1)}, u32[]{:S(2)}, u32[]{:S(2)}) collective-permute-start(bf16[256,1792]{1,0:T(8,128)(2,1)S(1)} %pad_maximum_fusion.refs_0_), channel_id=1, source_target_pairs={{0,12},{1,13},{2,14},{3,15},{4,0},{5,1},{6,2},{7,3},{8,4},{9,5},{1... | collective-permute-start | bytes 2752520 | tf_op jit(solution)/shard_map/ppermute | solution.py:27
  9.4 22.5 %collective-permute-start.5 = (bf16[256,1792]{1,0:T(8,128)(2,1)S(1)}, bf16[256,1792]{1,0:T(8,128)(2,1)S(1)}, u32[]{:S(2)}, u32[]{:S(2)}) collective-permute-start(bf16[256,1792]{1,0:T(8,128)(2,1)S(1)} %pad_maximum_fusion.refs_0_), channel_id=1, source_target_pairs={{0,17},{1,16},{2,19},{3,18},{4,21},{5,20},{6,23},{7,22},{8,25},{9,... | collective-permute-start | bytes 2752520 | tf_op jit(solution)/shard_map/ppermute | solution.py:27
  10.3 17.2 %collective-permute-start.1 = (bf16[1024,256]{1,0:T(8,128)(2,1)S(1)}, bf16[1024,256]{1,0:T(8,128)(2,1)S(1)}, u32[]{:S(2)}, u32[]{:S(2)}) collective-permute-start(bf16[1024,256]{1,0:T(8,128)(2,1)S(1)} %pad_maximum_fusion.2.refs_0_), channel_id=1, source_target_pairs={{0,32},{1,33},{2,34},{3,35},{4,36},{5,37},{6,38},{7,39},{8,40},{9,... | collective-permute-start | bytes 1572872 | tf_op jit(solution)/shard_map/ppermute | solution.py:27
  12.0 15.5 %collective-permute-start.2 = (bf16[1024,256]{1,0:T(8,128)(2,1)S(1)}, bf16[1024,256]{1,0:T(8,128)(2,1)S(1)}, u32[]{:S(2)}, u32[]{:S(2)}) collective-permute-start(bf16[1024,256]{1,0:T(8,128)(2,1)S(1)} %pad_maximum_fusion.2.refs_0_), channel_id=1, source_target_pairs={{0,224},{1,225},{2,226},{3,227},{4,228},{5,229},{6,230},{7,231},{8... | collective-permute-start | bytes 1572872 | tf_op jit(solution)/shard_map/ppermute | solution.py:27
  27.6 13.3 %collective-permute-start.8 = (bf16[1024,256]{1,0:T(8,128)(2,1)S(1)}, bf16[1024,256]{1,0:T(8,128)(2,1)S(1)}, u32[]{:S(2)}, u32[]{:S(2)}) collective-permute-start(bf16[1024,256]{1,0:T(8,128)(2,1)S(1)} %collective-permute-done.1.refs_1_), channel_id=1, source_target_pairs={{0,32},{1,33},{2,34},{3,35},{4,36},{5,37},{6,38},{7,39},{8,40},{9,... | collective-permute-start | bytes 1572872 | tf_op jit(solution)/shard_map/ppermute | solution.py:27
  27.6 13.3 %collective-permute-start.9 = (bf16[1024,256]{1,0:T(8,128)(2,1)S(1)}, bf16[1024,256]{1,0:T(8,128)(2,1)S(1)}, u32[]{:S(2)}, u32[]{:S(2)}) collective-permute-start(bf16[1024,256]{1,0:T(8,128)(2,1)S(1)} %collective-permute-done.2.refs_2_), channel_id=1, source_target_pairs={{0,224},{1,225},{2,226},{3,227},{4,228},{5,229},{6,230},{7,231},{8... | collective-permute-start | bytes 1572872 | tf_op jit(solution)/shard_map/ppermute | solution.py:27
  32.0 13.3 %collective-permute-start.6 = (bf16[256,1024]{1,0:T(8,128)(2,1)S(1)}, bf16[256,1024]{1,0:T(8,128)(2,1)S(1)}, u32[]{:S(2)}, u32[]{:S(2)}) collective-permute-start(bf16[256,1024]{1,0:T(8,128)(2,1)S(1)} %slice.36), channel_id=1, source_target_pairs={{0,4},{1,5},{2,6},{3,7},{4,8},{5,9},{6,10},{7,11},{8,12},{9,13},{1... | collective-permute-start | bytes 1572872 | tf_op jit(solution)/shard_map/ppermute | solution.py:27
  32.1 11.5 %collective-permute-start.7 = (bf16[256,768]{1,0:T(8,128)(2,1)S(1)}, bf16[256,768]{1,0:T(8,128)(2,1)S(1)}, u32[]{:S(2)}, u32[]{:S(2)}) collective-permute-start(bf16[256,768]{1,0:T(8,128)(2,1)S(1)} %slice.37), channel_id=1, source_target_pairs={{0,12},{1,13},{2,14},{3,15},{4,0},{5,1},{6,2},{7,3},{8,4},{9,5},{1... | collective-permute-start | bytes 1179656 | tf_op jit(solution)/shard_map/ppermute | solution.py:27
  40.9 12.4 %collective-permute-start.10 = (bf16[1024,256]{1,0:T(8,128)(2,1)S(1)}, bf16[1024,256]{1,0:T(8,128)(2,1)S(1)}, u32[]{:S(2)}, u32[]{:S(2)}) collective-permute-start(bf16[1024,256]{1,0:T(8,128)(2,1)S(1)} %collective-permute-done.8.refs_3_), channel_id=1, source_target_pairs={{0,32},{1,33},{2,34},{3,35},{4,36},{5,37},{6,38},{7,39},{8,40},{9,... | collective-permute-start | bytes 1572872 | tf_op jit(solution)/shard_map/ppermute | solution.py:27
  41.8 11.5 %collective-permute-start.11 = (bf16[1024,256]{1,0:T(8,128)(2,1)S(1)}, bf16[1024,256]{1,0:T(8,128)(2,1)S(1)}, u32[]{:S(2)}, u32[]{:S(2)}) collective-permute-start(bf16[1024,256]{1,0:T(8,128)(2,1)S(1)} %collective-permute-done.9.refs_4_), channel_id=1, source_target_pairs={{0,224},{1,225},{2,226},{3,227},{4,228},{5,229},{6,230},{7,231},{8... | collective-permute-start | bytes 1572872 | tf_op jit(solution)/shard_map/ppermute | solution.py:27
  45.2 22.8 %collective-permute-start.15 = (bf16[256,1792]{1,0:T(8,128)(2,1)S(1)}, bf16[256,1792]{1,0:T(8,128)(2,1)S(1)}, u32[]{:S(2)}, u32[]{:S(2)}) collective-permute-start(bf16[256,1792]{1,0:T(8,128)(2,1)S(1)} %collective-permute-done.5.refs_1_), channel_id=1, source_target_pairs={{0,4},{1,5},{2,6},{3,7},{4,8},{5,9},{6,10},{7,11},{8,12},{9,13},{1... | collective-permute-start | bytes 2752520 | tf_op jit(solution)/shard_map/ppermute | solution.py:27
  45.2 22.8 %collective-permute-start.16 = (bf16[256,1792]{1,0:T(8,128)(2,1)S(1)}, bf16[256,1792]{1,0:T(8,128)(2,1)S(1)}, u32[]{:S(2)}, u32[]{:S(2)}) collective-permute-start(bf16[256,1792]{1,0:T(8,128)(2,1)S(1)} %collective-permute-done.5.refs_1_), channel_id=1, source_target_pairs={{0,12},{1,13},{2,14},{3,15},{4,0},{5,1},{6,2},{7,3},{8,4},{9,5},{1... | collective-permute-start | bytes 2752520 | tf_op jit(solution)/shard_map/ppermute | solution.py:27
  47.9 13.4 %collective-permute-start.12 = (bf16[256,1024]{1,0:T(8,128)(2,1)S(1)}, bf16[256,1024]{1,0:T(8,128)(2,1)S(1)}, u32[]{:S(2)}, u32[]{:S(2)}) collective-permute-start(bf16[256,1024]{1,0:T(8,128)(2,1)S(1)} %collective-permute-done.6.refs_4_), channel_id=1, source_target_pairs={{0,17},{1,16},{2,19},{3,18},{4,21},{5,20},{6,23},{7,22},{8,25},{9,... | collective-permute-start | bytes 1572872 | tf_op jit(solution)/shard_map/ppermute | solution.py:27
  53.4 6.8 %collective-permute-start.13 = (bf16[512,256]{1,0:T(8,128)(2,1)S(1)}, bf16[512,256]{1,0:T(8,128)(2,1)S(1)}, u32[]{:S(2)}, u32[]{:S(2)}) collective-permute-start(bf16[512,256]{1,0:T(8,128)(2,1)S(1)} %slice.38), channel_id=1, source_target_pairs={{0,32},{1,33},{2,34},{3,35},{4,36},{5,37},{6,38},{7,39},{8,40},{9,... | collective-permute-start | bytes 786440 | tf_op jit(solution)/shard_map/ppermute | solution.py:27
  53.9 14.1 %collective-permute-start.17 = (bf16[256,768]{1,0:T(8,128)(2,1)S(1)}, bf16[256,768]{1,0:T(8,128)(2,1)S(1)}, u32[]{:S(2)}, u32[]{:S(2)}) collective-permute-start(bf16[256,768]{1,0:T(8,128)(2,1)S(1)} %collective-permute-done.7.refs_4_), channel_id=1, source_target_pairs={{0,17},{1,16},{2,19},{3,18},{4,21},{5,20},{6,23},{7,22},{8,25},{9,... | collective-permute-start | bytes 1179656 | tf_op jit(solution)/shard_map/ppermute | solution.py:27
  60.2 5.5 %collective-permute-start.14 = (bf16[512,256]{1,0:T(8,128)(2,1)S(1)}, bf16[512,256]{1,0:T(8,128)(2,1)S(1)}, u32[]{:S(2)}, u32[]{:S(2)}) collective-permute-start(bf16[512,256]{1,0:T(8,128)(2,1)S(1)} %slice.39), channel_id=1, source_target_pairs={{0,224},{1,225},{2,226},{3,227},{4,228},{5,229},{6,230},{7,231},{8... | collective-permute-start | bytes 786440 | tf_op jit(solution)/shard_map/ppermute | solution.py:27
  69.8 8.2 %collective-permute-start.18 = (bf16[2,512,384]{2,1,0:T(8,128)(2,1)S(1)}, bf16[2,512,384]{2,1,0:T(8,128)(2,1)S(1)}, u32[]{:S(2)}, u32[]{:S(2)}) collective-permute-start(bf16[2,512,384]{2,1,0:T(8,128)(2,1)S(1)} %shard_map.29), channel_id=1, source_target_pairs={{0,2},{1,3},{2,0},{3,1},{4,6},{5,7},{6,4},{7,5},{8,10},{9,11},{10,... | collective-permute-start | bytes 2359304 | tf_op jit(solution)/shard_map/ppermute | solution.py:27
  76.1 4.4 %collective-permute-start.19 = (bf16[2,512,512]{2,1,0:T(8,128)(2,1)S(1)}, bf16[2,512,512]{2,1,0:T(8,128)(2,1)S(1)}, u32[]{:S(2)}, u32[]{:S(2)}) collective-permute-start(bf16[2,512,512]{2,1,0:T(8,128)(2,1)S(1)} %shard_map.30), channel_id=1, source_target_pairs={{0,2},{1,3},{2,0},{3,1},{4,6},{5,7},{6,4},{7,5},{8,10},{9,11},{10,... | collective-permute-start | bytes 3145736 | tf_op jit(solution)/shard_map/ppermute | solution.py:27
  78.1 10.3 %collective-permute-start.21 = (bf16[512,384]{1,0:T(8,128)(2,1)S(1)}, bf16[512,384]{1,0:T(8,128)(2,1)S(1)}, u32[]{:S(2)}, u32[]{:S(2)}) collective-permute-start(bf16[512,384]{1,0:T(8,128)(2,1)S(1)} %fusion.9), channel_id=1, source_target_pairs={{0,1},{1,0},{2,3},{3,2},{4,5},{5,4},{6,7},{7,6},{8,9},{9,8},{10,11... | collective-permute-start | bytes 1179656 | tf_op jit(solution)/shard_map/ppermute | solution.py:27
  80.7 18.9 %collective-permute-start.20 = (bf16[512,512]{1,0:T(8,128)(2,1)S(1)}, bf16[512,512]{1,0:T(8,128)(2,1)S(1)}, u32[]{:S(2)}, u32[]{:S(2)}) collective-permute-start(bf16[512,512]{1,0:T(8,128)(2,1)S(1)} %fusion.8), channel_id=1, source_target_pairs={{0,1},{1,0},{2,3},{3,2},{4,5},{5,4},{6,7},{7,6},{8,9},{9,8},{10,11... | collective-permute-start | bytes 1572872 | tf_op jit(solution)/shard_map/ppermute | solution.py:27

commit v4 on v3

--- a/solution.py
+++ b/solution.py
@@ -90,14 +90,15 @@
     col = lax.axis_index("col")
     x_lo = lax.axis_index("depth")
     x_hi, y = col // (2 * Y), col // 2 % Y
-    for index, (side, dy, first) in enumerate(places):
+    for index, (side, dy, first, start, width) in enumerate(places):
         place = lax.rem(x_hi + side, X) * Y + lax.rem(y + dy, Y)
         term = jnp.dot(
             left[place, block * rows:(block + 1) * rows],
-            rights[index][:, first:first + 2 * share],
+            rights[index][:, first:first + width],
             preferred_element_type=jnp.float32,
         )
-        total[...] = total[...] + term if index else term
+        here = slice(start, start + width)
+        total[:, here] = total[:, here] + term if index else term
     for d in range(2):
         target[lax.rem(x_lo + d, 2)] = total[:, d * share:(d + 1) * share].astype(target.dtype)
 
@@ -143,7 +144,8 @@
     x_lo = lax.axis_index("depth")
     x_hi, core = col // (2 * Y), col % 2
     part = x_hi ^ x_lo
-    wide = -(-share // (2 * TILE)) * TILE
+    split = -(-share // (2 * TILE)) * 2 * TILE
+    wide = share - TILE
 
     def cut(first, width):
         return jnp.concatenate(
@@ -169,7 +171,7 @@
     move("d2", "d1", z_down)
 
     gate("u", "d", "n")
-    values["ua"], values["db"] = values["u"][:, :2 * wide], values["d"][:, 2 * wide:]
+    values["ua"], values["db"] = values["u"][:, :split], values["d"][:, split:]
     move("fa", "ua", y_up)
     move("fb", "db", y_down)
 
@@ -193,19 +195,31 @@
     gate("nfa", "u4")
     left = packed_left([(values[k], tuple(v)) for k, *v in a_pieces], rows)
     pieces, sizes, came = {}, {}, {}
-    for chunk, first in (("b", 2 * wide), ("a", 0)):
-        names = [("o", 0, 0, first), ("n", 1, 0, first), ("u", 0, Y - 1, first), ("d", 0, 1, first), ("f" + chunk, 0, 2, 0),
-                 ("nu", 1, Y - 1, first), ("nd", 1, 1, first), ("nf" + chunk, 1, 2, 0)]
+    for chunk, first, size in (("b", 2 * wide, columns - 2 * wide), ("a", 0, 2 * wide)):
+        names = []
+        for name, side, dy in (("o", 0, 0), ("n", 1, 0), ("u", 0, Y - 1), ("d", 0, 1), ("nu", 1, Y - 1), ("nd", 1, 1)):
+            names.append((name, side, dy, first, 0, size))
+        for name, side in (("f", 0), ("nf", 1)):
+            if first < split:
+                names.append((name + "a", side, 2, first, 0, min(size, split - first)))
+            if first + size > split:
+                start = max(split - first, 0)
+                names.append((name + "b", side, 2, first + start - split, start, size - start))
         pieces[chunk] = [(values[k], tuple(v)) for k, *v in names]
-        sizes[chunk] = values["f" + chunk].shape[1]
+        sizes[chunk] = size
         send = product(left, pieces[chunk], sizes[chunk], 1)
+        if came:
+            send, came["b"] = lax.optimization_barrier((send, came["b"]))
         came[chunk] = moved(send, sibling)
         left, _ = lax.optimization_barrier((left, send))
     parts = []
     for chunk in "ba":
         keep = product(left, pieces[chunk], sizes[chunk], 0)
         away = (keep[1] + came[chunk][1].astype(jnp.float32)).astype(jnp.bfloat16)
+        if parts:
+            away, before = lax.optimization_barrier((away, before))
         arrived = moved(away, x_pair)
+        before = arrived
         left, _ = lax.optimization_barrier((left, away))
         parts.append((keep[0] + came[chunk][0].astype(jnp.float32) + arrived.astype(jnp.float32)).astype(jnp.bfloat16))
     first = lax.pad(parts[0], jnp.zeros((), jnp.bfloat16), ((0, 0, 0), (wide, 0, 0)))

time: 101 us -> 101 us (level)
  waiting for transfers between devices: 54.7 us -> 56.2 us
  starting transfers between devices: 32.4 us -> 31.2 us
    ppermute x22, waiting for transfers between devices: 54.7 us -> 56.2 us  [moved(): return lax.ppermute(value, AXES, pairs)]
    ppermute x22, starting transfers between devices: 32.4 us -> 31.2 us  [moved(): return lax.ppermute(value, AXES, pairs)]
where the time goes in v4:
time: 101 us
  waiting for transfers between devices  56.2 us (56%)
  starting transfers between devices  31.2 us (31%)
  Pallas kernels  8.67 us (9%)
  local copies, waits for them, and re-layouts  3.31 us (3%)
  other arithmetic  1.57 us (2%)
    ppermute x22, waiting for transfers between devices, moved(): return lax.ppermute(value, AXES, pairs)  56.2 us
    ppermute x22, starting transfers between devices, moved(): return lax.ppermute(value, AXES, pairs)  31.2 us
    pallas_call x4, Pallas kernels, product(): pl.pallas_call(functools.partial(product_kernel, places, block), out_shap...  8.29 us
    dynamic_slice x2, local copies, waits for them, and re-layouts, cut(): lax.dynamic_slice(b_matrix, (part * half, d * share + first), (half, width))  2.13 us
  transfers between devices with their start and end apart: 22, of which 10 were waited for; matrix products, arithmetic and copies ran while one was open for 3% of the time, Pallas kernels for 7%

profile of v4, /device:TPU:1, one launch (start us, length us, event | category | flops | bytes accessed | tf_op | source)
XLA Modules:
  0.0 101.1 jit_solution(3047381920944902449)
XLA Ops:
  0.0 1.1 %constant_dynamic-slice_fusion.2 = (bf16[512,256]{1,0:T(8,128)(2,1)S(1)}, bf16[512,256]{1,0:T(8,128)(2,1)S(1)}) fusion(bf16[512,1024]{1,0:T(8,128)(2,1)} %param.2, s32[]{:T(128)S(6)} %select_n.25, s32[]{:T(128)S(6)} %select_n.26), kind=kLoop, calls=%fused_computation.19 | loop fusion | bytes 1048584 | tf_op jit(solution)/shard_map/dynamic_slice | solution.py:156
  1.1 3.3 %collective-permute-start = (bf16[512,256]{1,0:T(8,128)(2,1)S(1)}, bf16[512,256]{1,0:T(8,128)(2,1)S(1)}, u32[]{:S(2)}, u32[]{:S(2)}) collective-permute-start(bf16[512,256]{1,0:T(8,128)(2,1)S(1)} %get-tuple-element.64), channel_id=1, source_target_pairs={{0,2},{1,3},{2,0},{3,1},{4,6},{5,7},{6,4},{7,5},{8,10},{9,11},{10,... | collective-permute-start | bytes 786440 | tf_op jit(solution)/shard_map/ppermute | solution.py:27
  4.4 1.1 %constant_dynamic-slice_fusion = (bf16[256,640]{1,0:T(8,128)(2,1)S(1)}, bf16[256,640]{1,0:T(8,128)(2,1)S(1)}) fusion(bf16[512,1792]{1,0:T(8,128)(2,1)} %param.3, s32[]{:T(128)S(6)} %select_n.27), kind=kLoop, calls=%fused_computation.17 | loop fusion | bytes 1310724 | tf_op jit(solution)/shard_map/dynamic_slice | solution.py:152
  5.5 1.0 constant_dynamic-slice_fusion.4
  6.5 0.1 pad_maximum_fusion.refs_0_
  6.6 0.0 collective-permute-done
  6.6 0.1 collective-permute-start.3
  6.7 2.7 %collective-permute-start.4 = (bf16[256,1792]{1,0:T(8,128)(2,1)S(1)}, bf16[256,1792]{1,0:T(8,128)(2,1)S(1)}, u32[]{:S(2)}, u32[]{:S(2)}) collective-permute-start(bf16[256,1792]{1,0:T(8,128)(2,1)S(1)} %pad_maximum_fusion.refs_0_), channel_id=1, source_target_pairs={{0,12},{1,13},{2,14},{3,15},{4,0},{5,1},{6,2},{7,3},{8,4},{9,5},{1... | collective-permute-start | bytes 2752520 | tf_op jit(solution)/shard_map/ppermute | solution.py:27
  9.4 0.9 collective-permute-start.5
  10.3 1.7 %collective-permute-start.1 = (bf16[1024,256]{1,0:T(8,128)(2,1)S(1)}, bf16[1024,256]{1,0:T(8,128)(2,1)S(1)}, u32[]{:S(2)}, u32[]{:S(2)}) collective-permute-start(bf16[1024,256]{1,0:T(8,128)(2,1)S(1)} %pad_maximum_fusion.2.refs_0_), channel_id=1, source_target_pairs={{0,32},{1,33},{2,34},{3,35},{4,36},{5,37},{6,38},{7,39},{8,40},{9,... | collective-permute-start | bytes 1572872 | tf_op jit(solution)/shard_map/ppermute | solution.py:27
  12.0 4.0 %collective-permute-start.2 = (bf16[1024,256]{1,0:T(8,128)(2,1)S(1)}, bf16[1024,256]{1,0:T(8,128)(2,1)S(1)}, u32[]{:S(2)}, u32[]{:S(2)}) collective-permute-start(bf16[1024,256]{1,0:T(8,128)(2,1)S(1)} %pad_maximum_fusion.2.refs_0_), channel_id=1, source_target_pairs={{0,224},{1,225},{2,226},{3,227},{4,228},{5,229},{6,230},{7,231},{8... | collective-permute-start | bytes 1572872 | tf_op jit(solution)/shard_map/ppermute | solution.py:27
  16.0 11.5 %collective-permute-done.1.refs_1_ = bf16[1024,256]{1,0:T(8,128)(2,1)S(1)} collective-permute-done((bf16[1024,256]{1,0:T(8,128)(2,1)S(1)}, bf16[1024,256]{1,0:T(8,128)(2,1)S(1)}, u32[]{:S(2)}, u32[]{:S(2)}) %collective-permute-start.1) | collective-permute-done | bytes 524320 | tf_op jit(solution)/shard_map/ppermute | solution.py:27
  27.6 2.7 %collective-permute-start.9 = (bf16[1024,256]{1,0:T(8,128)(2,1)S(1)}, bf16[1024,256]{1,0:T(8,128)(2,1)S(1)}, u32[]{:S(2)}, u32[]{:S(2)}) collective-permute-start(bf16[1024,256]{1,0:T(8,128)(2,1)S(1)} %collective-permute-done.2.refs_2_), channel_id=1, source_target_pairs={{0,224},{1,225},{2,226},{3,227},{4,228},{5,229},{6,230},{7,231},{8... | collective-permute-start | bytes 1572872 | tf_op jit(solution)/shard_map/ppermute | solution.py:27
  30.2 0.0 collective-permute-done.4.refs_3_
  30.2 1.7 %collective-permute-done.5.refs_1_ = bf16[256,1792]{1,0:T(8,128)(2,1)S(1)} collective-permute-done((bf16[256,1792]{1,0:T(8,128)(2,1)S(1)}, bf16[256,1792]{1,0:T(8,128)(2,1)S(1)}, u32[]{:S(2)}, u32[]{:S(2)}) %collective-permute-start.5) | collective-permute-done | bytes 917536 | tf_op jit(solution)/shard_map/ppermute | solution.py:27
  31.9 0.1 slice.36
  32.0 0.1 collective-permute-start.6
  32.1 2.7 %collective-permute-start.7 = (bf16[256,768]{1,0:T(8,128)(2,1)S(1)}, bf16[256,768]{1,0:T(8,128)(2,1)S(1)}, u32[]{:S(2)}, u32[]{:S(2)}) collective-permute-start(bf16[256,768]{1,0:T(8,128)(2,1)S(1)} %slice.37), channel_id=1, source_target_pairs={{0,12},{1,13},{2,14},{3,15},{4,0},{5,1},{6,2},{7,3},{8,4},{9,5},{1... | collective-permute-start | bytes 1179656 | tf_op jit(solution)/shard_map/ppermute | solution.py:27
  34.8 6.1 %collective-permute-done.8.refs_3_ = bf16[1024,256]{1,0:T(8,128)(2,1)S(1)} collective-permute-done((bf16[1024,256]{1,0:T(8,128)(2,1)S(1)}, bf16[1024,256]{1,0:T(8,128)(2,1)S(1)}, u32[]{:S(2)}, u32[]{:S(2)}) %collective-permute-start.8) | collective-permute-done | bytes 524320 | tf_op jit(solution)/shard_map/ppermute | solution.py:27
  40.9 0.0 collective-permute-done.9.refs_4_
  40.9 0.9 collective-permute-start.10
  41.8 1.8 %collective-permute-start.11 = (bf16[1024,256]{1,0:T(8,128)(2,1)S(1)}, bf16[1024,256]{1,0:T(8,128)(2,1)S(1)}, u32[]{:S(2)}, u32[]{:S(2)}) collective-permute-start(bf16[1024,256]{1,0:T(8,128)(2,1)S(1)} %collective-permute-done.9.refs_4_), channel_id=1, source_target_pairs={{0,224},{1,225},{2,226},{3,227},{4,228},{5,229},{6,230},{7,231},{8... | collective-permute-start | bytes 1572872 | tf_op jit(solution)/shard_map/ppermute | solution.py:27
  43.6 1.6 %collective-permute-done.6.refs_6_ = bf16[256,1024]{1,0:T(8,128)(2,1)S(1)} collective-permute-done((bf16[256,1024]{1,0:T(8,128)(2,1)S(1)}, bf16[256,1024]{1,0:T(8,128)(2,1)S(1)}, u32[]{:S(2)}, u32[]{:S(2)}) %collective-permute-start.6) | collective-permute-done | bytes 524320 | tf_op jit(solution)/shard_map/ppermute | solution.py:27
  45.2 2.7 %collective-permute-start.16 = (bf16[256,1792]{1,0:T(8,128)(2,1)S(1)}, bf16[256,1792]{1,0:T(8,128)(2,1)S(1)}, u32[]{:S(2)}, u32[]{:S(2)}) collective-permute-start(bf16[256,1792]{1,0:T(8,128)(2,1)S(1)} %collective-permute-done.5.refs_1_), channel_id=1, source_target_pairs={{0,12},{1,13},{2,14},{3,15},{4,0},{5,1},{6,2},{7,3},{8,4},{9,5},{1... | collective-permute-start | bytes 2752520 | tf_op jit(solution)/shard_map/ppermute | solution.py:27
  47.9 1.2 %collective-permute-start.12 = (bf16[256,1024]{1,0:T(8,128)(2,1)S(1)}, bf16[256,1024]{1,0:T(8,128)(2,1)S(1)}, u32[]{:S(2)}, u32[]{:S(2)}) collective-permute-start(bf16[256,1024]{1,0:T(8,128)(2,1)S(1)} %collective-permute-done.6.refs_6_), channel_id=1, source_target_pairs={{0,17},{1,16},{2,19},{3,18},{4,21},{5,20},{6,23},{7,22},{8,25},{9,... | collective-permute-start | bytes 1572872 | tf_op jit(solution)/shard_map/ppermute | solution.py:27
  49.1 4.2 %collective-permute-done.10.refs_5_ = bf16[1024,256]{1,0:T(8,128)(2,1)S(1)} collective-permute-done((bf16[1024,256]{1,0:T(8,128)(2,1)S(1)}, bf16[1024,256]{1,0:T(8,128)(2,1)S(1)}, u32[]{:S(2)}, u32[]{:S(2)}) %collective-permute-start.10) | collective-permute-done | bytes 524320 | tf_op jit(solution)/shard_map/ppermute | solution.py:27
  53.4 0.5 collective-permute-start.13
  53.9 0.2 collective-permute-start.17
  54.1 6.0 %collective-permute-done.13.refs_7_ = bf16[512,256]{1,0:T(8,128)(2,1)S(1)} collective-permute-done((bf16[512,256]{1,0:T(8,128)(2,1)S(1)}, bf16[512,256]{1,0:T(8,128)(2,1)S(1)}, u32[]{:S(2)}, u32[]{:S(2)}) %collective-permute-start.13) | collective-permute-done | bytes 262176 | tf_op jit(solution)/shard_map/ppermute | solution.py:27
  60.2 1.2 %collective-permute-start.14 = (bf16[512,256]{1,0:T(8,128)(2,1)S(1)}, bf16[512,256]{1,0:T(8,128)(2,1)S(1)}, u32[]{:S(2)}, u32[]{:S(2)}) collective-permute-start(bf16[512,256]{1,0:T(8,128)(2,1)S(1)} %slice.39), channel_id=1, source_target_pairs={{0,224},{1,225},{2,226},{3,227},{4,228},{5,229},{6,230},{7,231},{8... | collective-permute-start | bytes 786440 | tf_op jit(solution)/shard_map/ppermute | solution.py:27
  61.3 4.3 %collective-permute-done.14.refs_8_ = bf16[512,256]{1,0:T(8,128)(2,1)S(1)} collective-permute-done((bf16[512,256]{1,0:T(8,128)(2,1)S(1)}, bf16[512,256]{1,0:T(8,128)(2,1)S(1)}, u32[]{:S(2)}, u32[]{:S(2)}) %collective-permute-start.14) | collective-permute-done | bytes 262176 | tf_op jit(solution)/shard_map/ppermute | solution.py:27
  65.7 0.4 shard_map.28.left
  66.1 2.0 %collective-permute-done.17.refs_7_.refs_9_ = bf16[256,768]{1,0:T(8,128)(2,1)S(1)} collective-permute-done((bf16[256,768]{1,0:T(8,128)(2,1)S(1)}, bf16[256,768]{1,0:T(8,128)(2,1)S(1)}, u32[]{:S(2)}, u32[]{:S(2)}) %collective-permute-start.17) | collective-permute-done | bytes 393248 | tf_op jit(solution)/shard_map/ppermute | solution.py:27
  68.0 1.2 %shard_map.29 = bf16[2,512,256]{2,1,0:T(8,128)(2,1)S(1)} custom-call(bf16[8,1024,256]{2,1,0:T(8,128)(2,1)S(1)} %shard_map.28.left, bf16[256,1792]{1,0:T(8,128)(2,1)S(1)} %pad_maximum_fusion.refs_0_, bf16[256,1792]{1,0:T(8,128)(2,1)S(1)} %collective-permute-done.5.refs_1_, bf16[256,1792]{1,0:T(8,128)(2,1)S(1)} %collective-permute-done.3.refs_2_, ...), custom_call_target="tpu_custom_call" | custom-call | flops 1073741824 | bytes 4194304 | tf_op jit(solution)/shard_map/pallas_call | solution.py:110
  69.3 3.9 %collective-permute-start.18 = (bf16[2,512,256]{2,1,0:T(8,128)(2,1)S(1)}, bf16[2,512,256]{2,1,0:T(8,128)(2,1)S(1)}, u32[]{:S(2)}, u32[]{:S(2)}) collective-permute-start(bf16[2,512,256]{2,1,0:T(8,128)(2,1)S(1)} %shard_map.29), channel_id=1, source_target_pairs={{0,2},{1,3},{2,0},{3,1},{4,6},{5,7},{6,4},{7,5},{8,10},{9,11},{10,... | collective-permute-start | bytes 1572872 | tf_op jit(solution)/shard_map/ppermute | solution.py:27
  73.2 2.9 %shard_map.30 = bf16[2,512,640]{2,1,0:T(8,128)(2,1)S(1)} custom-call(bf16[8,1024,256]{2,1,0:T(8,128)(2,1)S(1)} %shard_map.28.left, bf16[256,1792]{1,0:T(8,128)(2,1)S(1)} %pad_maximum_fusion.refs_0_, bf16[256,1792]{1,0:T(8,128)(2,1)S(1)} %collective-permute-done.5.refs_1_, bf16[256,1792]{1,0:T(8,128)(2,1)S(1)} %collective-permute-done.3.refs_2_, ...), custom_call_target="tpu_custom_call" | custom-call | flops 2684354560 | bytes 7340032 | tf_op jit(solution)/shard_map/pallas_call | solution.py:110
  76.1 0.1 collective-permute-start.19
  76.2 1.2 %shard_map.31 = f32[2,512,256]{2,1,0:T(8,128)S(1)} custom-call(bf16[8,1024,256]{2,1,0:T(8,128)(2,1)S(1)} %shard_map.28.left, bf16[256,1792]{1,0:T(8,128)(2,1)S(1)} %pad_maximum_fusion.refs_0_, bf16[256,1792]{1,0:T(8,128)(2,1)S(1)} %collective-permute-done.5.refs_1_, bf16[256,1792]{1,0:T(8,128)(2,1)S(1)} %collective-permute-done.3.refs_2_, ...), custom_call_target="tpu_custom_call" | custom-call | flops 1073741824 | bytes 4194304 | tf_op jit(solution)/shard_map/pallas_call | solution.py:110
  77.5 0.1 fusion.9
  77.6 0.1 collective-permute-start.20
  77.7 2.9 %shard_map.32 = f32[2,512,640]{2,1,0:T(8,128)S(1)} custom-call(bf16[8,1024,256]{2,1,0:T(8,128)(2,1)S(1)} %shard_map.28.left, bf16[256,1792]{1,0:T(8,128)(2,1)S(1)} %pad_maximum_fusion.refs_0_, bf16[256,1792]{1,0:T(8,128)(2,1)S(1)} %collective-permute-done.5.refs_1_, bf16[256,1792]{1,0:T(8,128)(2,1)S(1)} %collective-permute-done.3.refs_2_, ...), custom_call_target="tpu_custom_call" | custom-call | flops 2684354560 | bytes 7340032 | tf_op jit(solution)/shard_map/pallas_call | solution.py:110
  80.6 0.1 fusion.4
  80.7 4.3 %collective-permute-done.20 = bf16[512,256]{1,0:T(8,128)(2,1)S(1)} collective-permute-done((bf16[512,256]{1,0:T(8,128)(2,1)S(1)}, bf16[512,256]{1,0:T(8,128)(2,1)S(1)}, u32[]{:S(2)}, u32[]{:S(2)}) %collective-permute-start.20) | collective-permute-done | bytes 262176 | tf_op jit(solution)/shard_map/ppermute | solution.py:27
  85.0 0.3 collective-permute-start.21
  85.4 0.1 fusion.7
  85.4 14.5 %collective-permute-done.21 = bf16[512,640]{1,0:T(8,128)(2,1)S(1)} collective-permute-done((bf16[512,640]{1,0:T(8,128)(2,1)S(1)}, bf16[512,640]{1,0:T(8,128)(2,1)S(1)}, u32[]{:S(2)}, u32[]{:S(2)}) %collective-permute-start.21) | collective-permute-done | bytes 655392 | tf_op jit(solution)/shard_map/ppermute | solution.py:27
  99.9 0.2 fusion.3
  100.1 1.0 pad_maximum_fusion.1
  (15 shorter events, 0.1 us)
Async XLA Ops:
  1.1 5.5 %collective-permute-start = (bf16[512,256]{1,0:T(8,128)(2,1)S(1)}, bf16[512,256]{1,0:T(8,128)(2,1)S(1)}, u32[]{:S(2)}, u32[]{:S(2)}) collective-permute-start(bf16[512,256]{1,0:T(8,128)(2,1)S(1)} %get-tuple-element.64), channel_id=1, source_target_pairs={{0,2},{1,3},{2,0},{3,1},{4,6},{5,7},{6,4},{7,5},{8,10},{9,11},{10,... | collective-permute-start | bytes 786440 | tf_op jit(solution)/shard_map/ppermute | solution.py:27
  6.6 23.6 %collective-permute-start.3 = (bf16[256,1792]{1,0:T(8,128)(2,1)S(1)}, bf16[256,1792]{1,0:T(8,128)(2,1)S(1)}, u32[]{:S(2)}, u32[]{:S(2)}) collective-permute-start(bf16[256,1792]{1,0:T(8,128)(2,1)S(1)} %pad_maximum_fusion.refs_0_), channel_id=1, source_target_pairs={{0,4},{1,5},{2,6},{3,7},{4,8},{5,9},{6,10},{7,11},{8,12},{9,13},{1... | collective-permute-start | bytes 2752520 | tf_op jit(solution)/shard_map/ppermute | solution.py:27
  6.7 23.5 %collective-permute-start.4 = (bf16[256,1792]{1,0:T(8,128)(2,1)S(1)}, bf16[256,1792]{1,0:T(8,128)(2,1)S(1)}, u32[]{:S(2)}, u32[]{:S(2)}) collective-permute-start(bf16[256,1792]{1,0:T(8,128)(2,1)S(1)} %pad_maximum_fusion.refs_0_), channel_id=1, source_target_pairs={{0,12},{1,13},{2,14},{3,15},{4,0},{5,1},{6,2},{7,3},{8,4},{9,5},{1... | collective-permute-start | bytes 2752520 | tf_op jit(solution)/shard_map/ppermute | solution.py:27
  9.4 22.5 %collective-permute-start.5 = (bf16[256,1792]{1,0:T(8,128)(2,1)S(1)}, bf16[256,1792]{1,0:T(8,128)(2,1)S(1)}, u32[]{:S(2)}, u32[]{:S(2)}) collective-permute-start(bf16[256,1792]{1,0:T(8,128)(2,1)S(1)} %pad_maximum_fusion.refs_0_), channel_id=1, source_target_pairs={{0,17},{1,16},{2,19},{3,18},{4,21},{5,20},{6,23},{7,22},{8,25},{9,... | collective-permute-start | bytes 2752520 | tf_op jit(solution)/shard_map/ppermute | solution.py:27
  10.3 17.2 %collective-permute-start.1 = (bf16[1024,256]{1,0:T(8,128)(2,1)S(1)}, bf16[1024,256]{1,0:T(8,128)(2,1)S(1)}, u32[]{:S(2)}, u32[]{:S(2)}) collective-permute-start(bf16[1024,256]{1,0:T(8,128)(2,1)S(1)} %pad_maximum_fusion.2.refs_0_), channel_id=1, source_target_pairs={{0,32},{1,33},{2,34},{3,35},{4,36},{5,37},{6,38},{7,39},{8,40},{9,... | collective-permute-start | bytes 1572872 | tf_op jit(solution)/shard_map/ppermute | solution.py:27
  12.0 15.5 %collective-permute-start.2 = (bf16[1024,256]{1,0:T(8,128)(2,1)S(1)}, bf16[1024,256]{1,0:T(8,128)(2,1)S(1)}, u32[]{:S(2)}, u32[]{:S(2)}) collective-permute-start(bf16[1024,256]{1,0:T(8,128)(2,1)S(1)} %pad_maximum_fusion.2.refs_0_), channel_id=1, source_target_pairs={{0,224},{1,225},{2,226},{3,227},{4,228},{5,229},{6,230},{7,231},{8... | collective-permute-start | bytes 1572872 | tf_op jit(solution)/shard_map/ppermute | solution.py:27
  27.6 13.3 %collective-permute-start.8 = (bf16[1024,256]{1,0:T(8,128)(2,1)S(1)}, bf16[1024,256]{1,0:T(8,128)(2,1)S(1)}, u32[]{:S(2)}, u32[]{:S(2)}) collective-permute-start(bf16[1024,256]{1,0:T(8,128)(2,1)S(1)} %collective-permute-done.1.refs_1_), channel_id=1, source_target_pairs={{0,32},{1,33},{2,34},{3,35},{4,36},{5,37},{6,38},{7,39},{8,40},{9,... | collective-permute-start | bytes 1572872 | tf_op jit(solution)/shard_map/ppermute | solution.py:27
  27.6 13.3 %collective-permute-start.9 = (bf16[1024,256]{1,0:T(8,128)(2,1)S(1)}, bf16[1024,256]{1,0:T(8,128)(2,1)S(1)}, u32[]{:S(2)}, u32[]{:S(2)}) collective-permute-start(bf16[1024,256]{1,0:T(8,128)(2,1)S(1)} %collective-permute-done.2.refs_2_), channel_id=1, source_target_pairs={{0,224},{1,225},{2,226},{3,227},{4,228},{5,229},{6,230},{7,231},{8... | collective-permute-start | bytes 1572872 | tf_op jit(solution)/shard_map/ppermute | solution.py:27
  32.0 13.3 %collective-permute-start.6 = (bf16[256,1024]{1,0:T(8,128)(2,1)S(1)}, bf16[256,1024]{1,0:T(8,128)(2,1)S(1)}, u32[]{:S(2)}, u32[]{:S(2)}) collective-permute-start(bf16[256,1024]{1,0:T(8,128)(2,1)S(1)} %slice.36), channel_id=1, source_target_pairs={{0,4},{1,5},{2,6},{3,7},{4,8},{5,9},{6,10},{7,11},{8,12},{9,13},{1... | collective-permute-start | bytes 1572872 | tf_op jit(solution)/shard_map/ppermute | solution.py:27
  32.1 11.5 %collective-permute-start.7 = (bf16[256,768]{1,0:T(8,128)(2,1)S(1)}, bf16[256,768]{1,0:T(8,128)(2,1)S(1)}, u32[]{:S(2)}, u32[]{:S(2)}) collective-permute-start(bf16[256,768]{1,0:T(8,128)(2,1)S(1)} %slice.37), channel_id=1, source_target_pairs={{0,12},{1,13},{2,14},{3,15},{4,0},{5,1},{6,2},{7,3},{8,4},{9,5},{1... | collective-permute-start | bytes 1179656 | tf_op jit(solution)/shard_map/ppermute | solution.py:27
  40.9 12.4 %collective-permute-start.10 = (bf16[1024,256]{1,0:T(8,128)(2,1)S(1)}, bf16[1024,256]{1,0:T(8,128)(2,1)S(1)}, u32[]{:S(2)}, u32[]{:S(2)}) collective-permute-start(bf16[1024,256]{1,0:T(8,128)(2,1)S(1)} %collective-permute-done.8.refs_3_), channel_id=1, source_target_pairs={{0,32},{1,33},{2,34},{3,35},{4,36},{5,37},{6,38},{7,39},{8,40},{9,... | collective-permute-start | bytes 1572872 | tf_op jit(solution)/shard_map/ppermute | solution.py:27
  41.8 11.5 %collective-permute-start.11 = (bf16[1024,256]{1,0:T(8,128)(2,1)S(1)}, bf16[1024,256]{1,0:T(8,128)(2,1)S(1)}, u32[]{:S(2)}, u32[]{:S(2)}) collective-permute-start(bf16[1024,256]{1,0:T(8,128)(2,1)S(1)} %collective-permute-done.9.refs_4_), channel_id=1, source_target_pairs={{0,224},{1,225},{2,226},{3,227},{4,228},{5,229},{6,230},{7,231},{8... | collective-permute-start | bytes 1572872 | tf_op jit(solution)/shard_map/ppermute | solution.py:27
  45.2 22.8 %collective-permute-start.15 = (bf16[256,1792]{1,0:T(8,128)(2,1)S(1)}, bf16[256,1792]{1,0:T(8,128)(2,1)S(1)}, u32[]{:S(2)}, u32[]{:S(2)}) collective-permute-start(bf16[256,1792]{1,0:T(8,128)(2,1)S(1)} %collective-permute-done.5.refs_1_), channel_id=1, source_target_pairs={{0,4},{1,5},{2,6},{3,7},{4,8},{5,9},{6,10},{7,11},{8,12},{9,13},{1... | collective-permute-start | bytes 2752520 | tf_op jit(solution)/shard_map/ppermute | solution.py:27
  45.2 22.8 %collective-permute-start.16 = (bf16[256,1792]{1,0:T(8,128)(2,1)S(1)}, bf16[256,1792]{1,0:T(8,128)(2,1)S(1)}, u32[]{:S(2)}, u32[]{:S(2)}) collective-permute-start(bf16[256,1792]{1,0:T(8,128)(2,1)S(1)} %collective-permute-done.5.refs_1_), channel_id=1, source_target_pairs={{0,12},{1,13},{2,14},{3,15},{4,0},{5,1},{6,2},{7,3},{8,4},{9,5},{1... | collective-permute-start | bytes 2752520 | tf_op jit(solution)/shard_map/ppermute | solution.py:27
  47.9 13.4 %collective-permute-start.12 = (bf16[256,1024]{1,0:T(8,128)(2,1)S(1)}, bf16[256,1024]{1,0:T(8,128)(2,1)S(1)}, u32[]{:S(2)}, u32[]{:S(2)}) collective-permute-start(bf16[256,1024]{1,0:T(8,128)(2,1)S(1)} %collective-permute-done.6.refs_6_), channel_id=1, source_target_pairs={{0,17},{1,16},{2,19},{3,18},{4,21},{5,20},{6,23},{7,22},{8,25},{9,... | collective-permute-start | bytes 1572872 | tf_op jit(solution)/shard_map/ppermute | solution.py:27
  53.4 6.8 %collective-permute-start.13 = (bf16[512,256]{1,0:T(8,128)(2,1)S(1)}, bf16[512,256]{1,0:T(8,128)(2,1)S(1)}, u32[]{:S(2)}, u32[]{:S(2)}) collective-permute-start(bf16[512,256]{1,0:T(8,128)(2,1)S(1)} %slice.38), channel_id=1, source_target_pairs={{0,32},{1,33},{2,34},{3,35},{4,36},{5,37},{6,38},{7,39},{8,40},{9,... | collective-permute-start | bytes 786440 | tf_op jit(solution)/shard_map/ppermute | solution.py:27
  53.9 14.1 %collective-permute-start.17 = (bf16[256,768]{1,0:T(8,128)(2,1)S(1)}, bf16[256,768]{1,0:T(8,128)(2,1)S(1)}, u32[]{:S(2)}, u32[]{:S(2)}) collective-permute-start(bf16[256,768]{1,0:T(8,128)(2,1)S(1)} %collective-permute-done.7.refs_6_.refs_7_), channel_id=1, source_target_pairs={{0,17},{1,16},{2,19},{3,18},{4,21},{5,20},{6,23},{7,22},{8,25},{9,... | collective-permute-start | bytes 1179656 | tf_op jit(solution)/shard_map/ppermute | solution.py:27
  60.2 5.5 %collective-permute-start.14 = (bf16[512,256]{1,0:T(8,128)(2,1)S(1)}, bf16[512,256]{1,0:T(8,128)(2,1)S(1)}, u32[]{:S(2)}, u32[]{:S(2)}) collective-permute-start(bf16[512,256]{1,0:T(8,128)(2,1)S(1)} %slice.39), channel_id=1, source_target_pairs={{0,224},{1,225},{2,226},{3,227},{4,228},{5,229},{6,230},{7,231},{8... | collective-permute-start | bytes 786440 | tf_op jit(solution)/shard_map/ppermute | solution.py:27
  69.3 6.8 %collective-permute-start.18 = (bf16[2,512,256]{2,1,0:T(8,128)(2,1)S(1)}, bf16[2,512,256]{2,1,0:T(8,128)(2,1)S(1)}, u32[]{:S(2)}, u32[]{:S(2)}) collective-permute-start(bf16[2,512,256]{2,1,0:T(8,128)(2,1)S(1)} %shard_map.29), channel_id=1, source_target_pairs={{0,2},{1,3},{2,0},{3,1},{4,6},{5,7},{6,4},{7,5},{8,10},{9,11},{10,... | collective-permute-start | bytes 1572872 | tf_op jit(solution)/shard_map/ppermute | solution.py:27
  76.1 4.4 %collective-permute-start.19 = (bf16[2,512,640]{2,1,0:T(8,128)(2,1)S(1)}, bf16[2,512,640]{2,1,0:T(8,128)(2,1)S(1)}, u32[]{:S(2)}, u32[]{:S(2)}) collective-permute-start(bf16[2,512,640]{2,1,0:T(8,128)(2,1)S(1)} %shard_map.30), channel_id=1, source_target_pairs={{0,2},{1,3},{2,0},{3,1},{4,6},{5,7},{6,4},{7,5},{8,10},{9,11},{10,... | collective-permute-start | bytes 3932168 | tf_op jit(solution)/shard_map/ppermute | solution.py:27
  77.6 7.5 %collective-permute-start.20 = (bf16[512,256]{1,0:T(8,128)(2,1)S(1)}, bf16[512,256]{1,0:T(8,128)(2,1)S(1)}, u32[]{:S(2)}, u32[]{:S(2)}) collective-permute-start(bf16[512,256]{1,0:T(8,128)(2,1)S(1)} %fusion.9), channel_id=1, source_target_pairs={{0,1},{1,0},{2,3},{3,2},{4,5},{5,4},{6,7},{7,6},{8,9},{9,8},{10,11... | collective-permute-start | bytes 786440 | tf_op jit(solution)/shard_map/ppermute | solution.py:27
  85.0 14.9 %collective-permute-start.21 = (bf16[512,640]{1,0:T(8,128)(2,1)S(1)}, bf16[512,640]{1,0:T(8,128)(2,1)S(1)}, u32[]{:S(2)}, u32[]{:S(2)}) collective-permute-start(bf16[512,640]{1,0:T(8,128)(2,1)S(1)} %fusion.4), channel_id=1, source_target_pairs={{0,1},{1,0},{2,3},{3,2},{4,5},{5,4},{6,7},{7,6},{8,9},{9,8},{10,11... | collective-permute-start | bytes 1966088 | tf_op jit(solution)/shard_map/ppermute | solution.py:27
